TPU v7x, 512 devices: a whole 4x4x16 slice. The times are simulated.
512 devices in a mesh: ia: 64 (over x, z_lo, core), ja: 8 (over y, z_hi).
Axes of the slice: x: 4, y: 4, z: 16 (z_hi: 2, z_lo: 8; z = z_hi * 8 + z_lo), core: 2. Of those that a mesh axis runs over, the one named last changes fastest.
Arguments:
- state: bfloat16 [64, 2048, 384], P('ja', 'ia')
- cotangent: bfloat16 [64, 2048, 384], P('ja', 'ia'), may hold values from -6 to 6
- ocean: int32 [64, 2048], P('ja', 'ia'), may hold values from 0 to 1, as said below
- fold_partner: int32 [64], P('ia'), may hold values from 0 to 63, as said below
- kernel: float32 [49, 384], replicated, may hold values from -0.875 to 0.875
- ln_gain: float32 [384], replicated, may hold values from 0.25 to 1.75
- ln_shift: float32 [384], replicated, may hold values from -3 to 3
- w_up: bfloat16 [384, 768], replicated, may hold values from -0.3125 to 0.3125
- b_up: float32 [768], replicated, may hold values from -3 to 3
- w_down: bfloat16 [384, 768], replicated, may hold values from -0.21875 to 0.21875
- b_down: float32 [384], replicated, may hold values from -3 to 3
- layer_scale: float32 [384], replicated, may hold values from 0.5 to 2
Outputs:
- grad_state: bfloat16 [64, 2048, 384], P('ja', 'ia')
- grad_w_up: float32 [384, 768], P('ja', 'ia')
- grad_w_down: float32 [384, 768], P('ja', 'ia')
- grad_kernel: float32 [49, 384], replicated
- grad_channels: float32 [4, 384], replicated
- grad_b_up: float32 [768], replicated
Inputs may be any that keep to these rules, and one draw needn't show every extreme that they name: Within aligned tiles of 8 rows by 32 columns each cell is ocean with a probability drawn per tile from 0, 1/4, 1/2, 3/4 and 1. fold_partner[s] = (K - s) mod 64 for one K.
All inputs are finite; a program needn't handle non-finite values.
Results may differ from a plain program's by a relative error of at most 0.0063.
Values may be sent and summed in bfloat16 or wider, within the bound.
A program may use at most 64 MiB of HBM per device.

v0:
```python
import math

import jax
import jax.numpy as jnp
from jax import lax
from jax.sharding import PartitionSpec as P

KWIDTH = 7


def from_partner(value, axis, bit):
    mask = 2**bit
    pairs = [(source, source ^ mask) for source in range(lax.axis_size(axis))]
    return lax.ppermute(value, axis, pairs)


def shifted_2(block, axis, distance):
    devices = range(lax.axis_size(axis))
    route = [((i - distance) % len(devices), i) for i in devices]
    return lax.ppermute(block, axis, route)


def with_halo(block, sides, width, periodic):
    for axis, dim in sides:
        count = lax.axis_size(axis)
        forward = [(i, i + 1) for i in range(count - 1)]
        if periodic:
            forward.append((count - 1, 0))
        backward = [(target, source) for source, target in forward]
        low = lax.ppermute(
            lax.slice_in_dim(block, block.shape[dim] - width, None, axis=dim), axis, forward
        )
        high = lax.ppermute(lax.slice_in_dim(block, 0, width, axis=dim), axis, backward)
        block = jnp.concatenate([low, block, high], axis=dim)
    return block


def gelu_parts(pre):
    coeff = 0.7978845608028654
    inner = coeff * (pre + 0.044715 * pre * pre * pre)
    tanh_value = jnp.tanh(inner)
    value = 0.5 * pre * (1.0 + tanh_value)
    slope = 0.5 * (1.0 + tanh_value) + 0.5 * pre * (1.0 - tanh_value * tanh_value) * coeff * (
        1.0 + 3.0 * 0.044715 * pre * pre
    )
    return (value, slope)


def depthwise(padded, taps, rows, cols):
    total = jnp.zeros((rows, cols, padded.shape[2]), jnp.float32)
    for first in range(KWIDTH):
        for second in range(KWIDTH):
            total = (
                total
                + padded[first : first + rows, second : second + cols].astype(jnp.float32)
                * taps[first * KWIDTH + second]
            )
    return total


def block_grads(
    padded,
    cotangent,
    ocean,
    kernel,
    ln_gain,
    ln_shift,
    w_up,
    b_up,
    w_down,
    b_down,
    layer_scale,
    rows,
    cols,
):
    chans = padded.shape[2]
    cells = rows * cols
    conv = depthwise(padded, kernel, rows, cols).reshape(cells, chans)
    centred = conv - jnp.mean(conv, axis=1, keepdims=True)
    rstd = lax.rsqrt(jnp.mean(centred * centred, axis=1, keepdims=True) + 1e-06)
    unit = centred * rstd
    normed = (unit * ln_gain + ln_shift).astype(jnp.bfloat16)
    pre = jnp.dot(normed, w_up, preferred_element_type=jnp.float32) + b_up
    act, slope = gelu_parts(pre)
    hidden = act.astype(jnp.bfloat16)
    branch = (
        lax.dot_general(
            hidden, w_down, (((1,), (1,)), ((), ())), preferred_element_type=jnp.float32
        )
        + b_down
    )
    masked = cotangent.reshape(cells, chans).astype(jnp.float32) * ocean.reshape(cells, 1).astype(
        jnp.float32
    )
    d_branch = masked * layer_scale
    d_branch_b = d_branch.astype(jnp.bfloat16)
    g_scale = jnp.sum(masked * branch, axis=0)
    g_bdown = jnp.sum(d_branch, axis=0)
    g_wdown = lax.dot_general(
        d_branch_b, hidden, (((0,), (0,)), ((), ())), preferred_element_type=jnp.float32
    )
    d_hidden = jnp.dot(d_branch_b, w_down, preferred_element_type=jnp.float32)
    d_pre = d_hidden * slope
    d_pre_b = d_pre.astype(jnp.bfloat16)
    g_bup = jnp.sum(d_pre, axis=0)
    g_wup = lax.dot_general(
        normed, d_pre_b, (((0,), (0,)), ((), ())), preferred_element_type=jnp.float32
    )
    d_normed = lax.dot_general(
        d_pre_b, w_up, (((1,), (1,)), ((), ())), preferred_element_type=jnp.float32
    )
    g_gain = jnp.sum(d_normed * unit, axis=0)
    g_shift = jnp.sum(d_normed, axis=0)
    scaled = d_normed * ln_gain
    d_conv = rstd * (
        scaled
        - jnp.mean(scaled, axis=1, keepdims=True)
        - unit * jnp.mean(scaled * unit, axis=1, keepdims=True)
    )
    d_conv_b = d_conv.astype(jnp.bfloat16).reshape(rows, cols, chans)
    d_conv_f = d_conv_b.astype(jnp.float32)
    g_kernel = jnp.stack(
        [
            jnp.sum(
                padded[first : first + rows, second : second + cols].astype(jnp.float32) * d_conv_f,
                axis=(0, 1),
            )
            for first in range(KWIDTH)
            for second in range(KWIDTH)
        ]
    )
    g_chan = jnp.stack([g_gain, g_shift, g_bdown, g_scale])
    return (d_conv_b, g_wup, g_wdown, g_kernel, g_chan, g_bup)


def mirror(strip, offset, lanes, swap_step, shift_step):
    digits = lanes.bit_length() - 1
    moved = strip
    for bit in range(digits):
        moved = swap_step(moved, bit)
    for bit in range(digits):
        shifted = shift_step(moved, 1 << bit)
        moved = jnp.where(offset // (1 << bit) % 2 == 1, shifted, moved)
    return moved


def swap_state(part, bit):
    return from_partner(part, "ia", bit)


def shift_state(part, step):
    return shifted_2(part, "ia", step)


def swap_ghost(part, bit):
    return from_partner(part.astype(jnp.bfloat16), "ia", bit).astype(part.dtype)


def shift_ghost(part, step):
    return shifted_2(part.astype(jnp.bfloat16), "ia", step).astype(part.dtype)


def local(
    state,
    cotangent,
    ocean,
    fold_partner,
    kernel,
    ln_gain,
    ln_shift,
    w_up,
    b_up,
    w_down,
    b_down,
    layer_scale,
):
    rows, cols, chans = state.shape
    pad = KWIDTH // 2
    lanes = lax.axis_size("ia")
    bands = lax.axis_size("ja")
    on_top = lax.axis_index("ja") == bands - 1
    offset = (fold_partner[0] + lax.axis_index("ia") + 1) % lanes
    factor = 1.0 / math.sqrt(rows * bands * cols * lanes)
    wide = with_halo(state, (("ia", 1),), pad, True)
    tall = with_halo(wide, (("ja", 0),), pad, False)
    strip = wide[rows - 1 - pad : rows - 1]
    arrived = mirror(strip, offset, lanes, swap_state, shift_state)
    ghost = jnp.where(on_top, arrived[::-1, ::-1], tall[rows + pad :])
    padded = jnp.concatenate([tall[: rows + pad], ghost], axis=0)
    d_conv, g_wup, g_wdown, g_kernel, g_chan, g_bup = block_grads(
        padded,
        cotangent,
        ocean,
        kernel,
        ln_gain,
        ln_shift,
        w_up,
        b_up,
        w_down,
        b_down,
        layer_scale,
        rows,
        cols,
    )
    grad_kernel, grad_channels, grad_b_up = lax.psum(
        (g_kernel * factor, g_chan * factor, g_bup * factor), ("ia", "ja")
    )
    up_term = g_wup * factor
    down_term = g_wdown * factor
    up_part, down_part = (
        lax.psum_scatter(up_term, "ia", scatter_dimension=1, tiled=True),
        lax.psum_scatter(down_term, "ia", scatter_dimension=1, tiled=True),
    )
    grad_w_up, grad_w_down = (
        lax.psum_scatter(up_part, "ja", scatter_dimension=0, tiled=True),
        lax.psum_scatter(down_part, "ja", scatter_dimension=0, tiled=True),
    )
    d_wide = with_halo(d_conv, (("ia", 1),), pad, True)
    d_tall = with_halo(d_wide, (("ja", 0),), pad, False)
    flipped = kernel[::-1]
    extended = jnp.concatenate(
        [d_tall, jnp.zeros((pad, cols + 2 * pad, chans), jnp.bfloat16)], axis=0
    )
    back = depthwise(extended, flipped, rows + pad, cols)
    main = back[:rows]
    incoming = mirror(back[rows:], offset, lanes, swap_ghost, shift_ghost)
    fold = jnp.where(on_top, incoming[::-1, ::-1], jnp.zeros_like(incoming))
    total = cotangent.astype(jnp.float32) + main
    total = jnp.concatenate(
        [total[: rows - 1 - pad], total[rows - 1 - pad : rows - 1] + fold, total[rows - 1 :]],
        axis=0,
    )
    grad_state = total.astype(jnp.bfloat16)
    return (grad_state, grad_w_up, grad_w_down, grad_kernel, grad_channels, grad_b_up)


def solution(mesh):
    placed = (
        P("ja", "ia", None),
        P("ja", "ia", None),
        P("ja", "ia"),
        P("ia"),
        P(),
        P(),
        P(),
        P(),
        P(),
        P(),
        P(),
        P(),
    )
    return jax.shard_map(
        local,
        mesh=mesh,
        in_specs=placed,
        out_specs=(P("ja", "ia", None), P("ja", "ia"), P("ja", "ia"), P(), P(), P()),
        check_vma=False,
    )
```

profile of v0, /device:TPU:1, one launch (start us, length us, event | category | flops | bytes accessed | tf_op | source)
XLA Modules:
  0.0 1087.6 jit_solution(6672874421611215497)
XLA Ops:
  9.0 4.9 collective-permute-start
  13.9 5.8 collective-permute-start.1
  21.6 13.2 %collective-permute-start.3 = (bf16[3,38,384]{2,1,0:T(8,128)(2,1)S(1)}, bf16[3,38,384]{2,1,0:T(8,128)(2,1)S(1)}, u32[]{:S(2)}, u32[]{:S(2)}) collective-permute-start(bf16[3,38,384]{2,1,0:T(8,128)(2,1)S(1)} %get-tuple-element.140), channel_id=1, source_target_pairs={{0,8},{8,0},{16,24},{24,16},{32,40},{40,32},{48,56},{56,48},{64,72... | collective-permute-start | bytes 262664 | tf_op jit(solution)/shard_map/ppermute | solution.py:14
  37.6 3.9 collective-permute-done.4
  43.4 7.1 collective-permute-done.5
  52.4 12.4 %collective-permute-done.6 = bf16[3,38,384]{2,1,0:T(8,128)(2,1)S(1)} collective-permute-done((bf16[3,38,384]{2,1,0:T(8,128)(2,1)S(1)}, bf16[3,38,384]{2,1,0:T(8,128)(2,1)S(1)}, u32[]{:S(2)}, u32[]{:S(2)}) %collective-permute-start.6) | collective-permute-done | bytes 87584 | tf_op jit(solution)/shard_map/ppermute | solution.py:14
  66.7 3.7 collective-permute-done.7
  70.4 3.7 collective-permute-start.8
  77.2 3.2 collective-permute-start.9
  84.4 12.7 %collective-permute-done.10 = bf16[3,38,384]{2,1,0:T(8,128)(2,1)S(1)} collective-permute-done((bf16[3,38,384]{2,1,0:T(8,128)(2,1)S(1)}, bf16[3,38,384]{2,1,0:T(8,128)(2,1)S(1)}, u32[]{:S(2)}, u32[]{:S(2)}) %collective-permute-start.10) | collective-permute-done | bytes 87584 | tf_op jit(solution)/shard_map/ppermute | solution.py:20
  99.1 11.7 %collective-permute-done.11 = bf16[3,38,384]{2,1,0:T(8,128)(2,1)S(1)} collective-permute-done((bf16[3,38,384]{2,1,0:T(8,128)(2,1)S(1)}, bf16[3,38,384]{2,1,0:T(8,128)(2,1)S(1)}, u32[]{:S(2)}, u32[]{:S(2)}) %collective-permute-start.11) | collective-permute-done | bytes 87584 | tf_op jit(solution)/shard_map/ppermute | solution.py:20
  112.8 9.7 collective-permute-done.12
  124.4 14.1 %collective-permute-start.2 = (bf16[3,38,384]{2,1,0:T(8,128)(2,1)S(1)}, bf16[3,38,384]{2,1,0:T(8,128)(2,1)S(1)}, u32[]{:S(2)}, u32[]{:S(2)}) collective-permute-start(bf16[3,38,384]{2,1,0:T(8,128)(2,1)S(1)} %get-tuple-element.139), channel_id=1, source_target_pairs={{0,1},{1,2},{2,3},{3,4},{4,5},{5,6},{6,7},{8,9},{9,10},{10,11},{11... | collective-permute-start | bytes 262664 | tf_op jit(solution)/shard_map/ppermute | solution.py:30
  139.9 4.5 collective-permute-start.14
  146.9 5.8 collective-permute-done.15
  152.8 3.4 fusion.120
  162.4 5.7 collective-permute-start.16
  168.1 13.4 %collective-permute-start.17 = (bf16[8,3,384]{2,1,0:T(4,128)(2,1)S(1)}, bf16[8,3,384]{2,1,0:T(4,128)(2,1)S(1)}, u32[]{:S(2)}, u32[]{:S(2)}) collective-permute-start(bf16[8,3,384]{2,1,0:T(4,128)(2,1)S(1)} %get-tuple-element.144), channel_id=1, source_target_pairs={{8,0},{16,8},{24,16},{32,24},{40,32},{48,40},{56,48},{64,56},{72,6... | collective-permute-start | bytes 55304 | tf_op jit(solution)/shard_map/ppermute | solution.py:33
  182.4 7.3 collective-permute-start.18
  191.1 7.3 collective-permute-done.18
  198.4 5.3 collective-permute-done.19
  204.0 4.0 multiply_add_fusion.1
  208.1 14.5 %collective-permute-start.20 = (bf16[3,32,384]{2,1,0:T(8,128)(2,1)S(1)}, bf16[3,32,384]{2,1,0:T(8,128)(2,1)S(1)}, u32[]{:S(2)}, u32[]{:S(2)}) collective-permute-start(bf16[3,32,384]{2,1,0:T(8,128)(2,1)S(1)} %slice.1182), channel_id=1, source_target_pairs={{0,8},{8,0},{16,24},{24,16},{32,40},{40,32},{48,56},{56,48},{64,72... | collective-permute-start | bytes 221192 | tf_op jit(solution)/shard_map/ppermute | solution.py:14
  226.4 3.5 collective-permute-done.21
  231.9 228.5 %fusion.117 = (f32[384,16]{0,1:T(8,128)S(1)}, f32[384,16]{0,1:T(8,128)S(1)}) fusion(f32[384,768]{0,1:T(8,128)S(1)} %convolution_multiply_fusion.1, f32[384,768]{0,1:T(8,128)} %convolution_multiply_fusion), kind=kCustom, calls=%all-reduce-scatter.2 | all-reduce-scatter fusion | flops 786433 | bytes 2410496
  464.4 4.0 collective-permute-start.45
  468.4 10.7 collective-permute-start.62
  486.3 10.3 collective-permute-start.57
  502.6 7.7 collective-permute-start.55
  512.9 3.4 collective-permute-start.53
  516.3 6.3 collective-permute-start.52
  538.1 10.8 collective-permute-start.44
  551.0 6.0 collective-permute-start.42
  557.0 6.7 collective-permute-start.41
  567.2 4.7 concatenate.106
  574.5 3.1 collective-permute-start.39
  577.6 5.2 collective-permute-start.38
  582.8 5.8 collective-permute-start.37
  589.9 3.7 collective-permute-start.35
  600.6 3.6 collective-permute-start.27
  607.8 7.3 collective-permute-done.27
  618.0 10.5 collective-permute-done.28
  630.6 91.2 %reduce-scatter.13.cloned.1.call-done = f32[48,12]{1,0:T(8,128)} async-done(((f32[384,12]{1,0:T(8,128)}), f32[48,12]{1,0:T(8,128)}) %reduce-scatter.13.cloned.1.call-update) | async-done | bytes 2320
  723.2 103.7 %reduce-scatter.11.cloned.1.call-done = f32[48,12]{1,0:T(8,128)} async-done(((f32[384,12]{1,0:T(8,128)}), f32[48,12]{1,0:T(8,128)}) %reduce-scatter.11.cloned.1.call-update) | async-done | bytes 2320
  831.6 3.2 collective-permute-done.30
  834.8 3.7 collective-permute-start.31
  838.5 102.1 %all-reduce.4 = (f32[4,384]{1,0:T(4,128)}, f32[768]{0:T(1024)}) all-reduce(f32[4,384]{1,0:T(4,128)S(1)} %maximum_multiply_fusion, f32[768]{0:T(1024)S(1)} %broadcast_multiply_fusion.1), channel_id=1, replica_groups=mesh['ia'=64,'ja'=8] {'ia','ja'}, use_global_device_ids=true, to_apply=%region_62.63 | all-reduce | flops 2304 | bytes 18432 | tf_op jit(solution)/shard_map/psum | solution.py:205
  941.5 137.2 %all-reduce.8.cloned.1.call-done = f32[49,384]{1,0:T(8,128)} async-done(((f32[49,384]{1,0:T(8,128)}), f32[49,384]{1,0:T(8,128)}) %all-reduce.8.cloned.1.call-update) | async-done | bytes 75280 | tf_op jit(solution)/shard_map/psum | solution.py:205
  (319 shorter events, 108.8 us)
Async XLA Ops:
  8.0 713.7 %reduce-scatter.13.cloned.1.call-start = ((), (), s32[]{:S(2)}) async-start(), calls=%async_computation.4 | async-start | bytes 221184
  21.6 14.1 %collective-permute-start.3 = (bf16[3,38,384]{2,1,0:T(8,128)(2,1)S(1)}, bf16[3,38,384]{2,1,0:T(8,128)(2,1)S(1)}, u32[]{:S(2)}, u32[]{:S(2)}) collective-permute-start(bf16[3,38,384]{2,1,0:T(8,128)(2,1)S(1)} %get-tuple-element.140), channel_id=1, source_target_pairs={{0,8},{8,0},{16,24},{24,16},{32,40},{40,32},{48,56},{56,48},{64,72... | collective-permute-start | bytes 262664 | tf_op jit(solution)/shard_map/ppermute | solution.py:14
  50.5 14.3 %collective-permute-start.6 = (bf16[3,38,384]{2,1,0:T(8,128)(2,1)S(1)}, bf16[3,38,384]{2,1,0:T(8,128)(2,1)S(1)}, u32[]{:S(2)}, u32[]{:S(2)}) collective-permute-start(bf16[3,38,384]{2,1,0:T(8,128)(2,1)S(1)} %collective-permute-done.5), channel_id=1, source_target_pairs={{0,64},{8,72},{16,80},{24,88},{32,96},{40,104},{48,112},{56,120},{... | collective-permute-start | bytes 262664 | tf_op jit(solution)/shard_map/ppermute | solution.py:14
  82.3 14.7 %collective-permute-start.10 = (bf16[3,38,384]{2,1,0:T(8,128)(2,1)S(1)}, bf16[3,38,384]{2,1,0:T(8,128)(2,1)S(1)}, u32[]{:S(2)}, u32[]{:S(2)}) collective-permute-start(bf16[3,38,384]{2,1,0:T(8,128)(2,1)S(1)} %broadcast_select_fusion), channel_id=1, source_target_pairs={{496,0},{504,8},{0,16},{8,24},{16,32},{24,40},{32,48},{40,56},{48,... | collective-permute-start | bytes 262664 | tf_op jit(solution)/shard_map/ppermute | solution.py:20
  97.1 13.7 %collective-permute-start.11 = (bf16[3,38,384]{2,1,0:T(8,128)(2,1)S(1)}, bf16[3,38,384]{2,1,0:T(8,128)(2,1)S(1)}, u32[]{:S(2)}, u32[]{:S(2)}) collective-permute-start(bf16[3,38,384]{2,1,0:T(8,128)(2,1)S(1)} %broadcast_select_fusion.1), channel_id=1, source_target_pairs={{480,0},{488,8},{496,16},{504,24},{0,32},{8,40},{16,48},{24,56},{3... | collective-permute-start | bytes 262664 | tf_op jit(solution)/shard_map/ppermute | solution.py:20
  122.4 17.4 %collective-permute-start.13 = (bf16[3,38,384]{2,1,0:T(8,128)(2,1)S(1)}, bf16[3,38,384]{2,1,0:T(8,128)(2,1)S(1)}, u32[]{:S(2)}, u32[]{:S(2)}) collective-permute-start(bf16[3,38,384]{2,1,0:T(8,128)(2,1)S(1)} %broadcast_select_fusion.3), channel_id=1, source_target_pairs={{384,0},{392,8},{400,16},{408,24},{416,32},{424,40},{432,48},{440,... | collective-permute-start | bytes 262664 | tf_op jit(solution)/shard_map/ppermute | solution.py:20
  124.4 28.2 %collective-permute-start.2 = (bf16[3,38,384]{2,1,0:T(8,128)(2,1)S(1)}, bf16[3,38,384]{2,1,0:T(8,128)(2,1)S(1)}, u32[]{:S(2)}, u32[]{:S(2)}) collective-permute-start(bf16[3,38,384]{2,1,0:T(8,128)(2,1)S(1)} %get-tuple-element.139), channel_id=1, source_target_pairs={{0,1},{1,2},{2,3},{3,4},{4,5},{5,6},{6,7},{8,9},{9,10},{10,11},{11... | collective-permute-start | bytes 262664 | tf_op jit(solution)/shard_map/ppermute | solution.py:30
  138.5 14.1 %collective-permute-start.15 = (bf16[3,38,384]{2,1,0:T(8,128)(2,1)S(1)}, bf16[3,38,384]{2,1,0:T(8,128)(2,1)S(1)}, u32[]{:S(2)}, u32[]{:S(2)}) collective-permute-start(bf16[3,38,384]{2,1,0:T(8,128)(2,1)S(1)} %get-tuple-element.141), channel_id=1, source_target_pairs={{1,0},{2,1},{3,2},{4,3},{5,4},{6,5},{7,6},{9,8},{10,9},{11,10},{12... | collective-permute-start | bytes 262664 | tf_op jit(solution)/shard_map/ppermute | solution.py:33
  162.4 19.1 %collective-permute-start.16 = (bf16[8,3,384]{2,1,0:T(4,128)(2,1)S(1)}, bf16[8,3,384]{2,1,0:T(4,128)(2,1)S(1)}, u32[]{:S(2)}, u32[]{:S(2)}) collective-permute-start(bf16[8,3,384]{2,1,0:T(4,128)(2,1)S(1)} %get-tuple-element.143), channel_id=1, source_target_pairs={{0,8},{8,16},{16,24},{24,32},{32,40},{40,48},{48,56},{56,64},{64,7... | collective-permute-start | bytes 55304 | tf_op jit(solution)/shard_map/ppermute | solution.py:30
  168.1 14.2 %collective-permute-start.17 = (bf16[8,3,384]{2,1,0:T(4,128)(2,1)S(1)}, bf16[8,3,384]{2,1,0:T(4,128)(2,1)S(1)}, u32[]{:S(2)}, u32[]{:S(2)}) collective-permute-start(bf16[8,3,384]{2,1,0:T(4,128)(2,1)S(1)} %get-tuple-element.144), channel_id=1, source_target_pairs={{8,0},{16,8},{24,16},{32,24},{40,32},{48,40},{56,48},{64,56},{72,6... | collective-permute-start | bytes 55304 | tf_op jit(solution)/shard_map/ppermute | solution.py:33
  182.4 16.0 %collective-permute-start.18 = (bf16[3,38,384]{2,1,0:T(8,128)(2,1)S(1)}, bf16[3,38,384]{2,1,0:T(8,128)(2,1)S(1)}, u32[]{:S(2)}, u32[]{:S(2)}) collective-permute-start(bf16[3,38,384]{2,1,0:T(8,128)(2,1)S(1)} %get-tuple-element.135), channel_id=1, source_target_pairs={{0,1},{1,2},{2,3},{3,4},{4,5},{5,6},{6,7},{8,9},{9,10},{10,11},{11... | collective-permute-start | bytes 262664 | tf_op jit(solution)/shard_map/ppermute | solution.py:30
  189.7 14.0 %collective-permute-start.19 = (bf16[3,38,384]{2,1,0:T(8,128)(2,1)S(1)}, bf16[3,38,384]{2,1,0:T(8,128)(2,1)S(1)}, u32[]{:S(2)}, u32[]{:S(2)}) collective-permute-start(bf16[3,38,384]{2,1,0:T(8,128)(2,1)S(1)} %get-tuple-element.136), channel_id=1, source_target_pairs={{1,0},{2,1},{3,2},{4,3},{5,4},{6,5},{7,6},{9,8},{10,9},{11,10},{12... | collective-permute-start | bytes 262664 | tf_op jit(solution)/shard_map/ppermute | solution.py:33
  208.1 16.0 %collective-permute-start.20 = (bf16[3,32,384]{2,1,0:T(8,128)(2,1)S(1)}, bf16[3,32,384]{2,1,0:T(8,128)(2,1)S(1)}, u32[]{:S(2)}, u32[]{:S(2)}) collective-permute-start(bf16[3,32,384]{2,1,0:T(8,128)(2,1)S(1)} %slice.1182), channel_id=1, source_target_pairs={{0,8},{8,0},{16,24},{24,16},{32,40},{40,32},{48,56},{56,48},{64,72... | collective-permute-start | bytes 221192 | tf_op jit(solution)/shard_map/ppermute | solution.py:14
  230.0 269.2 %collective-permute-start.22 = (bf16[3,32,384]{2,1,0:T(8,128)(2,1)}, bf16[3,32,384]{2,1,0:T(8,128)(2,1)}, u32[]{:S(2)}, u32[]{:S(2)}) collective-permute-start(bf16[3,32,384]{2,1,0:T(8,128)(2,1)} %collective-permute-done.21), channel_id=1, source_target_pairs={{0,32},{8,40},{16,48},{24,56},{32,0},{40,8},{48,16},{56,24},{64,96... | collective-permute-start | bytes 221192 | tf_op jit(solution)/shard_map/ppermute | solution.py:14
  460.4 20.0 %collective-permute-start.46 = (f32[384,16]{0,1:T(8,128)S(1)}, f32[384,16]{0,1:T(8,128)S(1)}, u32[]{:S(2)}, u32[]{:S(2)}) collective-permute-start(f32[384,16]{0,1:T(8,128)S(1)} %get-tuple-element.122), channel_id=1, source_target_pairs={{0,120},{8,128},{16,136},{24,144},{32,152},{40,160},{48,168},{56,1... | collective-permute-start | bytes 73736
  463.1 16.1 %collective-permute-start.47 = (f32[384,12]{0,1:T(8,128)S(1)}, f32[384,12]{0,1:T(8,128)S(1)}, u32[]{:S(2)}, u32[]{:S(2)}) collective-permute-start(f32[384,12]{0,1:T(8,128)S(1)} %slice.959), channel_id=1, source_target_pairs={{0,128},{8,136},{16,144},{24,152},{32,160},{40,168},{48,176},{56,1... | collective-permute-start | bytes 55304
  464.4 19.3 %collective-permute-start.45 = (f32[384,16]{0,1:T(8,128)S(1)}, f32[384,16]{0,1:T(8,128)S(1)}, u32[]{:S(2)}, u32[]{:S(2)}) collective-permute-start(f32[384,16]{0,1:T(8,128)S(1)} %get-tuple-element.122), channel_id=1, source_target_pairs={{0,112},{8,120},{16,128},{24,136},{32,144},{40,152},{48,160},{56,1... | collective-permute-start | bytes 73736
  468.4 16.6 %collective-permute-start.62 = (f32[384,16]{0,1:T(8,128)S(1)}, f32[384,16]{0,1:T(8,128)S(1)}, u32[]{:S(2)}, u32[]{:S(2)}) collective-permute-start(f32[384,16]{0,1:T(8,128)S(1)} %get-tuple-element.123), channel_id=1, source_target_pairs={{0,120},{8,128},{16,136},{24,144},{32,152},{40,160},{48,168},{56,1... | collective-permute-start | bytes 73736
  480.4 16.2 %collective-permute-start.60 = (f32[384,16]{0,1:T(8,128)S(1)}, f32[384,16]{0,1:T(8,128)S(1)}, u32[]{:S(2)}, u32[]{:S(2)}) collective-permute-start(f32[384,16]{0,1:T(8,128)S(1)} %get-tuple-element.123), channel_id=1, source_target_pairs={{0,104},{8,112},{16,120},{24,128},{32,136},{40,144},{48,152},{56,1... | collective-permute-start | bytes 73736
  483.7 18.9 %collective-permute-start.59 = (f32[384,16]{0,1:T(8,128)S(1)}, f32[384,16]{0,1:T(8,128)S(1)}, u32[]{:S(2)}, u32[]{:S(2)}) collective-permute-start(f32[384,16]{0,1:T(8,128)S(1)} %get-tuple-element.123), channel_id=1, source_target_pairs={{0,96},{8,104},{16,112},{24,120},{32,128},{40,136},{48,144},{56,15... | collective-permute-start | bytes 73736
  485.0 25.4 %collective-permute-start.58 = (f32[384,16]{0,1:T(8,128)S(1)}, f32[384,16]{0,1:T(8,128)S(1)}, u32[]{:S(2)}, u32[]{:S(2)}) collective-permute-start(f32[384,16]{0,1:T(8,128)S(1)} %get-tuple-element.123), channel_id=1, source_target_pairs={{0,88},{8,96},{16,104},{24,112},{32,120},{40,128},{48,136},{56,144... | collective-permute-start | bytes 73736
  486.3 26.6 %collective-permute-start.57 = (f32[384,16]{0,1:T(8,128)S(1)}, f32[384,16]{0,1:T(8,128)S(1)}, u32[]{:S(2)}, u32[]{:S(2)}) collective-permute-start(f32[384,16]{0,1:T(8,128)S(1)} %get-tuple-element.123), channel_id=1, source_target_pairs={{0,80},{8,88},{16,96},{24,104},{32,112},{40,120},{48,128},{56,136}... | collective-permute-start | bytes 73736
  496.7 19.6 %collective-permute-start.56 = (f32[384,16]{0,1:T(8,128)S(1)}, f32[384,16]{0,1:T(8,128)S(1)}, u32[]{:S(2)}, u32[]{:S(2)}) collective-permute-start(f32[384,16]{0,1:T(8,128)S(1)} %get-tuple-element.123), channel_id=1, source_target_pairs={{0,72},{8,80},{16,88},{24,96},{32,104},{40,112},{48,120},{56,128},... | collective-permute-start | bytes 73736
  499.2 23.4 %collective-permute-start.23 = (bf16[3,32,384]{2,1,0:T(8,128)(2,1)}, bf16[3,32,384]{2,1,0:T(8,128)(2,1)}, u32[]{:S(2)}, u32[]{:S(2)}) collective-permute-start(bf16[3,32,384]{2,1,0:T(8,128)(2,1)} %collective-permute-done.22), channel_id=1, source_target_pairs={{0,64},{8,72},{16,80},{24,88},{32,96},{40,104},{48,112},{56,120},{... | collective-permute-start | bytes 221192 | tf_op jit(solution)/shard_map/ppermute | solution.py:14
  502.6 23.6 %collective-permute-start.55 = (f32[384,16]{0,1:T(8,128)S(1)}, f32[384,16]{0,1:T(8,128)}, u32[]{:S(2)}, u32[]{:S(2)}) collective-permute-start(f32[384,16]{0,1:T(8,128)S(1)} %get-tuple-element.123), channel_id=1, source_target_pairs={{0,64},{8,72},{16,80},{24,88},{32,96},{40,104},{48,112},{56,120},{... | collective-permute-start | bytes 73736
  510.3 18.0 %collective-permute-start.54 = (f32[384,16]{0,1:T(8,128)S(1)}, f32[384,16]{0,1:T(8,128)}, u32[]{:S(2)}, u32[]{:S(2)}) collective-permute-start(f32[384,16]{0,1:T(8,128)S(1)} %get-tuple-element.123), channel_id=1, source_target_pairs={{0,56},{8,64},{16,72},{24,80},{32,88},{40,96},{48,104},{56,112},{6... | collective-permute-start | bytes 73736
  512.9 17.6 %collective-permute-start.53 = (f32[384,16]{0,1:T(8,128)S(1)}, f32[384,16]{0,1:T(8,128)}, u32[]{:S(2)}, u32[]{:S(2)}) collective-permute-start(f32[384,16]{0,1:T(8,128)S(1)} %get-tuple-element.123), channel_id=1, source_target_pairs={{0,48},{8,56},{16,64},{24,72},{32,80},{40,88},{48,96},{56,104},{64... | collective-permute-start | bytes 73736
  516.3 17.0 %collective-permute-start.52 = (f32[384,16]{0,1:T(8,128)S(1)}, f32[384,16]{0,1:T(8,128)}, u32[]{:S(2)}, u32[]{:S(2)}) collective-permute-start(f32[384,16]{0,1:T(8,128)S(1)} %get-tuple-element.123), channel_id=1, source_target_pairs={{0,40},{8,48},{16,56},{24,64},{32,72},{40,80},{48,88},{56,96},{64,... | collective-permute-start | bytes 73736
  528.3 20.5 %collective-permute-start.50 = (f32[384,16]{0,1:T(8,128)S(1)}, f32[384,16]{0,1:T(8,128)S(1)}, u32[]{:S(2)}, u32[]{:S(2)}) collective-permute-start(f32[384,16]{0,1:T(8,128)S(1)} %get-tuple-element.123), channel_id=1, source_target_pairs={{0,24},{8,32},{16,40},{24,48},{32,56},{40,64},{48,72},{56,80},{64,... | collective-permute-start | bytes 73736
  530.4 20.6 %collective-permute-start.49 = (f32[384,16]{0,1:T(8,128)S(1)}, f32[384,16]{0,1:T(8,128)S(1)}, u32[]{:S(2)}, u32[]{:S(2)}) collective-permute-start(f32[384,16]{0,1:T(8,128)S(1)} %get-tuple-element.123), channel_id=1, source_target_pairs={{0,16},{8,24},{16,32},{24,40},{32,48},{40,56},{48,64},{56,72},{64,... | collective-permute-start | bytes 73736
  533.3 23.8 %collective-permute-start.48 = (f32[384,16]{0,1:T(8,128)S(1)}, f32[384,16]{0,1:T(8,128)S(1)}, u32[]{:S(2)}, u32[]{:S(2)}) collective-permute-start(f32[384,16]{0,1:T(8,128)S(1)} %get-tuple-element.123), channel_id=1, source_target_pairs={{0,8},{8,16},{16,24},{24,32},{32,40},{40,48},{48,56},{56,64},{64,7... | collective-permute-start | bytes 73736
  535.5 28.2 %collective-permute-start.25 = (bf16[3,32,384]{2,1,0:T(8,128)(2,1)}, bf16[3,32,384]{2,1,0:T(8,128)(2,1)S(1)}, u32[]{:S(2)}, u32[]{:S(2)}) collective-permute-start(bf16[3,32,384]{2,1,0:T(8,128)(2,1)} %collective-permute-done.24), channel_id=1, source_target_pairs={{0,256},{8,264},{16,272},{24,280},{32,288},{40,296},{48,304},{56,3... | collective-permute-start | bytes 221192 | tf_op jit(solution)/shard_map/ppermute | solution.py:14
  538.1 33.8 %collective-permute-start.44 = (f32[384,16]{0,1:T(8,128)S(1)}, f32[384,16]{0,1:T(8,128)S(1)}, u32[]{:S(2)}, u32[]{:S(2)}) collective-permute-start(f32[384,16]{0,1:T(8,128)S(1)} %get-tuple-element.122), channel_id=1, source_target_pairs={{0,104},{8,112},{16,120},{24,128},{32,136},{40,144},{48,152},{56,1... | collective-permute-start | bytes 73736
  548.9 25.6 %collective-permute-start.43 = (f32[384,16]{0,1:T(8,128)S(1)}, f32[384,16]{0,1:T(8,128)S(1)}, u32[]{:S(2)}, u32[]{:S(2)}) collective-permute-start(f32[384,16]{0,1:T(8,128)S(1)} %get-tuple-element.122), channel_id=1, source_target_pairs={{0,96},{8,104},{16,112},{24,120},{32,128},{40,136},{48,144},{56,15... | collective-permute-start | bytes 73736
  551.0 26.6 %collective-permute-start.42 = (f32[384,16]{0,1:T(8,128)S(1)}, f32[384,16]{0,1:T(8,128)S(1)}, u32[]{:S(2)}, u32[]{:S(2)}) collective-permute-start(f32[384,16]{0,1:T(8,128)S(1)} %get-tuple-element.122), channel_id=1, source_target_pairs={{0,88},{8,96},{16,104},{24,112},{32,120},{40,128},{48,136},{56,144... | collective-permute-start | bytes 73736
  557.0 25.7 %collective-permute-start.41 = (f32[384,16]{0,1:T(8,128)S(1)}, f32[384,16]{0,1:T(8,128)S(1)}, u32[]{:S(2)}, u32[]{:S(2)}) collective-permute-start(f32[384,16]{0,1:T(8,128)S(1)} %get-tuple-element.122), channel_id=1, source_target_pairs={{0,80},{8,88},{16,96},{24,104},{32,112},{40,120},{48,128},{56,136}... | collective-permute-start | bytes 73736
  563.7 24.8 %collective-permute-start.26 = (bf16[3,32,384]{2,1,0:T(8,128)(2,1)S(1)}, bf16[3,32,384]{2,1,0:T(8,128)(2,1)S(1)}, u32[]{:S(2)}, u32[]{:S(2)}) collective-permute-start(bf16[3,32,384]{2,1,0:T(8,128)(2,1)S(1)} %collective-permute-done.25), channel_id=1, source_target_pairs={{504,0},{0,8},{8,16},{16,24},{24,32},{32,40},{40,48},{48,56},{56,6... | collective-permute-start | bytes 221192 | tf_op jit(solution)/shard_map/ppermute | solution.py:20
  571.9 17.9 %collective-permute-start.40 = (f32[384,16]{0,1:T(8,128)S(1)}, f32[384,16]{0,1:T(8,128)S(1)}, u32[]{:S(2)}, u32[]{:S(2)}) collective-permute-start(f32[384,16]{0,1:T(8,128)S(1)} %get-tuple-element.122), channel_id=1, source_target_pairs={{0,72},{8,80},{16,88},{24,96},{32,104},{40,112},{48,120},{56,128},... | collective-permute-start | bytes 73736
  574.5 19.1 %collective-permute-start.39 = (f32[384,16]{0,1:T(8,128)S(1)}, f32[384,16]{0,1:T(8,128)S(1)}, u32[]{:S(2)}, u32[]{:S(2)}) collective-permute-start(f32[384,16]{0,1:T(8,128)S(1)} %get-tuple-element.122), channel_id=1, source_target_pairs={{0,64},{8,72},{16,80},{24,88},{32,96},{40,104},{48,112},{56,120},{... | collective-permute-start | bytes 73736
  577.6 17.6 %collective-permute-start.38 = (f32[384,16]{0,1:T(8,128)S(1)}, f32[384,16]{0,1:T(8,128)S(1)}, u32[]{:S(2)}, u32[]{:S(2)}) collective-permute-start(f32[384,16]{0,1:T(8,128)S(1)} %get-tuple-element.122), channel_id=1, source_target_pairs={{0,56},{8,64},{16,72},{24,80},{32,88},{40,96},{48,104},{56,112},{6... | collective-permute-start | bytes 73736
  582.8 15.3 %collective-permute-start.37 = (f32[384,16]{0,1:T(8,128)S(1)}, f32[384,16]{0,1:T(8,128)S(1)}, u32[]{:S(2)}, u32[]{:S(2)}) collective-permute-start(f32[384,16]{0,1:T(8,128)S(1)} %get-tuple-element.122), channel_id=1, source_target_pairs={{0,48},{8,56},{16,64},{24,72},{32,80},{40,88},{48,96},{56,104},{64... | collective-permute-start | bytes 73736
  589.9 15.3 %collective-permute-start.35 = (f32[384,16]{0,1:T(8,128)S(1)}, f32[384,16]{0,1:T(8,128)S(1)}, u32[]{:S(2)}, u32[]{:S(2)}) collective-permute-start(f32[384,16]{0,1:T(8,128)S(1)} %get-tuple-element.122), channel_id=1, source_target_pairs={{0,32},{8,40},{16,48},{24,56},{32,64},{40,72},{48,80},{56,88},{64,... | collective-permute-start | bytes 73736
  600.6 14.6 %collective-permute-start.27 = (bf16[3,32,384]{2,1,0:T(8,128)(2,1)S(1)}, bf16[3,32,384]{2,1,0:T(8,128)(2,1)S(1)}, u32[]{:S(2)}, u32[]{:S(2)}) collective-permute-start(bf16[3,32,384]{2,1,0:T(8,128)(2,1)S(1)} %fusion.113), channel_id=1, source_target_pairs={{496,0},{504,8},{0,16},{8,24},{16,32},{24,40},{32,48},{40,56},{48,... | collective-permute-start | bytes 221192 | tf_op jit(solution)/shard_map/ppermute | solution.py:20
  605.1 221.8 %reduce-scatter.11.cloned.1.call-start = ((), (), s32[]{:S(2)}) async-start(), calls=%async_computation.3 | async-start | bytes 221184
  615.2 13.3 %collective-permute-start.28 = (bf16[3,32,384]{2,1,0:T(8,128)(2,1)S(1)}, bf16[3,32,384]{2,1,0:T(8,128)(2,1)S(1)}, u32[]{:S(2)}, u32[]{:S(2)}) collective-permute-start(bf16[3,32,384]{2,1,0:T(8,128)(2,1)S(1)} %fusion.116), channel_id=1, source_target_pairs={{480,0},{488,8},{496,16},{504,24},{0,32},{8,40},{16,48},{24,56},{3... | collective-permute-start | bytes 221192 | tf_op jit(solution)/shard_map/ppermute | solution.py:20
  618.0 460.7 %all-reduce.8.cloned.1.call-start = ((), (), s32[]{:S(2)}) async-start(), calls=%async_computation.2 | async-start | bytes 172032 | tf_op jit(solution)/shard_map/psum | solution.py:205
  628.6 199.7 %collective-permute-start.29 = (bf16[3,32,384]{2,1,0:T(8,128)(2,1)S(1)}, bf16[3,32,384]{2,1,0:T(8,128)(2,1)S(1)}, u32[]{:S(2)}, u32[]{:S(2)}) collective-permute-start(bf16[3,32,384]{2,1,0:T(8,128)(2,1)S(1)} %fusion.114), channel_id=1, source_target_pairs={{448,0},{456,8},{464,16},{472,24},{480,32},{488,40},{496,48},{504,... | collective-permute-start | bytes 221192 | tf_op jit(solution)/shard_map/ppermute | solution.py:20
  834.8 105.8 %collective-permute-start.31 = (bf16[3,32,384]{2,1,0:T(8,128)(2,1)S(1)}, bf16[3,32,384]{2,1,0:T(8,128)(2,1)S(1)}, u32[]{:S(2)}, u32[]{:S(2)}) collective-permute-start(bf16[3,32,384]{2,1,0:T(8,128)(2,1)S(1)} %fusion.115), channel_id=1, source_target_pairs={{256,0},{264,8},{272,16},{280,24},{288,32},{296,40},{304,48},{312,... | collective-permute-start | bytes 221192 | tf_op jit(solution)/shard_map/ppermute | solution.py:20
  (70 other events, 2225.8 us)
Sparse Core Ops, SparseCore 0:
  605.2 116.5 reduce-scatter.12
  727.4 99.4 reduce-scatter.10
Sparse Core Ops, SparseCore 1:
  630.7 447.9 all-reduce.7
where the time goes:
time: 1090 us
  waiting for transfers between devices  444 us (41%)
  blocking collectives  331 us (30%)
  starting transfers between devices  254 us (23%)
  between operations  19.2 us (2%)
  local copies, waits for them, and re-layouts  17.2 us (2%)
  other arithmetic  15 us (1%)
    unnamed x1, blocking collectives  229 us
    unnamed x37, waiting for transfers between devices  195 us
    psum x1, waiting for transfers between devices, local(): lax.psum((g_kernel * factor, g_chan * factor, g_bup * factor), ('ia', 'ja'))  137 us
    unnamed x34, starting transfers between devices  120 us
    psum x1, blocking collectives, local(): lax.psum((g_kernel * factor, g_chan * factor, g_bup * factor), ('ia', 'ja'))  102 us
    ppermute x12, waiting for transfers between devices, shifted_2(): return lax.ppermute(block, axis, route)  58.2 us
    ppermute x12, starting transfers between devices, from_partner(): return lax.ppermute(value, axis, pairs)  49 us
    ppermute x12, waiting for transfers between devices, from_partner(): return lax.ppermute(value, axis, pairs)  33.8 us
  transfers between devices with their start and end apart: 67, of which 23 were waited for; matrix products, arithmetic and copies ran while one was open for 23% of the time, Pallas kernels for 0%

commit v1 on v0

v1 whole, which is shorter than its diff:
```python
import functools
import math

import jax
import jax.numpy as jnp
from jax import lax
from jax.experimental import pallas as pl
from jax.experimental.pallas import tpu as pltpu
from jax.sharding import PartitionSpec as P

KW = 7
PAD = 3
ROWS = 8
COLS = 32
CH = 384
HID = 768
CELLS = ROWS * COLS
WIDE = 48
F32 = jnp.float32
BF16 = jnp.bfloat16
LANES = 64
BANDS = 8
COEFF = 0.7978845608028654
CUBIC = 0.044715
FACTOR = 1.0 / math.sqrt(ROWS * BANDS * COLS * LANES)


def place(x, y, z, c):
    return {"ia": x * 16 + lax.rem(z, 8) * 2 + c, "ja": y * 2 + z // 8}


def dot(a, b, dims=(1, 0)):
    return lax.dot_general(
        a, b, (((dims[0],), (dims[1],)), ((), ())), preferred_element_type=F32
    )


def sub8(v):
    return v[0:8] + v[8:16] + v[16:24] + v[24:32]


def onehot(rows, cols, target):
    want = target(lax.broadcasted_iota(jnp.int32, (1, cols), 1))
    here = lax.broadcasted_iota(jnp.int32, (rows, cols), 0)
    return jnp.where(here == want, 1.0, 0.0).astype(BF16)


def split3(v):
    hi = v.astype(BF16)
    rest = v - hi.astype(F32)
    mid = rest.astype(BF16)
    low = (rest - mid.astype(F32)).astype(BF16)
    zeros = jnp.zeros((13, v.shape[1]), F32)
    return jnp.concatenate(
        [hi.astype(F32), mid.astype(F32), low.astype(F32), zeros], axis=0
    ).astype(BF16)


def conv_into(wide, taps, flip, write):
    def tile(ct, _):
        lanes = pl.ds(pl.multiple_of(ct * 128, 128), 128)
        total = [jnp.zeros((COLS, 128), F32) for _ in range(ROWS)]
        for b in range(KW):
            weight = []
            for a in range(KW):
                tap = a * KW + b
                tap = KW * KW - 1 - tap if flip else tap
                weight.append(taps[tap : tap + 1, lanes])
            for r in range(ROWS + 2 * PAD):
                value = wide[ct, r, 5 + b : 5 + b + COLS, :]
                for a in range(KW):
                    j = r - a
                    if 0 <= j < ROWS:
                        total[j] = total[j] + value * weight[a]
        write(ct, lanes, total)
        return 0

    lax.fori_loop(0, 3, tile, 0)


def beyond_into(wide, taps, write):
    def tile(ct, _):
        lanes = pl.ds(pl.multiple_of(ct * 128, 128), 128)
        total = [jnp.zeros((COLS, 128), F32) for _ in range(PAD)]
        for b in range(KW):
            for a in range(4, KW):
                tap = a * KW + b
                weight = taps[tap : tap + 1, lanes]
                for j in range(PAD):
                    r = ROWS + j + 6 - a
                    if r <= ROWS + PAD - 1:
                        value = wide[ct, r, 11 - b : 11 - b + COLS, :]
                        total[j] = total[j] + value * weight
        write(lanes, total)
        return 0

    lax.fori_loop(0, 3, tile, 0)


def body(
    state, ghost, cot, ocean, taps_in, gain_in, shift_in, wup_in, bup_in, wdown_in, bdown_in, scale_in,
    gs_out, edge_out, beyond_out, tile_out, gk_out, gc_out, gb_out,
    xs, cs, oc, taps, gain, shift, wup0, bup0, wdown0, bdown, scale,
    hw, he, hv, cw, ce, dw, de, dv, ew, ee,
    wide, dwide, wup, wdown, bup, conv, unit, rstd, normed, masked, dbr, dhid, pre, hidden, dpre, dnorm, dcv, dcb,
    g, gc, h, h1, h2, r2, t, tz, perm,
    s, sc, s1, sx, s2, sy, s3, sz, b1, b2, b3,
    loc, hs, hr, qs, qr, ds, dr, es, er, cs_s, cs_r, f_s, f_r, k_s, k_r, z_s, z_r,
    sa_s, sa_r, sx_s, sx_r, sy_s, sy_r, sz_s, sz_r, gy_s, gy_r, gx_s, gx_r, gc_s, gc_r,
):
    ia, ja = lax.axis_index("ia"), lax.axis_index("ja")
    x, zl, c = ia // 16, lax.rem(ia // 2, 8), lax.rem(ia, 2)
    y, zh = ja // 2, lax.rem(ja, 2)
    z = zh * 8 + zl
    top, bottom = ja == BANDS - 1, ja == 0
    east = {"ia": lax.rem(ia + 1, LANES), "ja": ja}
    west = {"ia": lax.rem(ia + LANES - 1, LANES), "ja": ja}
    north = {"ia": ia, "ja": ja + 1}
    south = {"ia": ia, "ja": ja - 1}

    def remote(src, dst, send, recv, device):
        return pltpu.make_async_remote_copy(
            src_ref=src, dst_ref=dst, send_sem=send, recv_sem=recv,
            device_id=device, device_id_type=pl.DeviceIdType.MESH,
        )

    def peer_x(d):
        return place(lax.rem(x + d, 4), y, z, c)

    def peer_y(d):
        return place(x, lax.rem(y + d, 4), z, c)

    def peer_z(d):
        return place(x, y, lax.rem(z + d, 16), c)

    other = place(x, y, z, 1 - c)

    loads = [
        pltpu.make_async_copy(src, dst, loc.at[i])
        for i, (src, dst) in enumerate(
            [
                (state, xs), (cot, cs), (ocean, oc), (taps_in, taps), (gain_in, gain), (shift_in, shift),
                (wup_in, wup0), (bup_in, bup0), (wdown_in, wdown0), (bdown_in, bdown), (scale_in, scale),
            ]
        )
    ]
    for load in loads:
        load.start()

    barrier = pltpu.get_barrier_semaphore()

    def greet(device):
        pl.semaphore_signal(barrier, inc=1, device_id=device, device_id_type=pl.DeviceIdType.MESH)

    greet(east)
    greet(west)
    greet(other)
    for d in range(1, 4):
        greet(peer_x(d))
        greet(peer_y(d))
    for d in range(1, 16):
        greet(peer_z(d))

    greet({"ia": ia, "ja": lax.rem(ja + 1, BANDS)})
    greet({"ia": ia, "ja": lax.rem(ja + BANDS - 1, BANDS)})
    pl.semaphore_wait(barrier, 26)

    def halo(src, w, e, v, send, recv):
        to_north = remote(src.at[5:8], v.at[0], send.at[0], recv.at[0], north)
        to_south = remote(src.at[0:3], v.at[1], send.at[1], recv.at[1], south)
        to_east = remote(src.at[:, 16:32], w, send.at[2], recv.at[2], east)
        to_west = remote(src.at[:, 0:16], e, send.at[3], recv.at[3], west)

        @pl.when(jnp.logical_not(top))
        def _():
            to_north.start()

        @pl.when(jnp.logical_not(bottom))
        def _():
            to_south.start()

        to_east.start()
        to_west.start()
        return to_north, to_south, to_east, to_west

    def corners(v, w, e, send, recv):
        to_east = remote(v.at[:, :, 16:32], w, send.at[0], recv.at[0], east)
        to_west = remote(v.at[:, :, 0:16], e, send.at[1], recv.at[1], west)
        to_east.start()
        to_west.start()
        return to_east, to_west

    def finish_rows(copies):
        to_north, to_south, _, _ = copies

        @pl.when(jnp.logical_not(top))
        def _():
            to_north.wait_send()
            to_south.wait_recv()

        @pl.when(jnp.logical_not(bottom))
        def _():
            to_south.wait_send()
            to_north.wait_recv()

    def widen(dst, v, centre, w, e, v_w, v_e):
        for ct in range(3):
            lanes = slice(ct * 128, ct * 128 + 128)
            for r in range(ROWS):
                dst[ct, PAD + r, 0:8, :] = w[r, :, lanes].astype(F32)[8:16]
                dst[ct, PAD + r, 40:48, :] = e[r, :, lanes].astype(F32)[0:8]
                if centre is not None:
                    dst[ct, PAD + r, 8:40, :] = centre[r, :, lanes].astype(F32)
            for k in range(2):
                for q in range(PAD):
                    r = q + k * (ROWS + PAD)
                    dst[ct, r, 0:8, :] = v_w[k, q, :, lanes].astype(F32)[8:16]
                    dst[ct, r, 40:48, :] = v_e[k, q, :, lanes].astype(F32)[0:8]
                    dst[ct, r, 8:40, :] = v[k, q, :, lanes].astype(F32)

    first = halo(state, hw, he, hv, hs, hr)

    for load in loads:
        load.wait()

    @pl.when(top)
    def _():
        copy = pltpu.make_async_copy(ghost, hv.at[1], loc.at[11])
        copy.start()
        copy.wait()

    @pl.when(bottom)
    def _():
        hv[0] = jnp.zeros((PAD, COLS, CH), BF16)

    def old(p):
        return (p % 384) // 96 * 192 + (p % 96) // 12 * 24 + p // 384 * 12 + p % 12

    perm[...] = onehot(HID, HID, old)
    wup[...] = dot(wup0[...], perm[...]).astype(BF16)
    wdown[...] = dot(wdown0[...], perm[...]).astype(BF16)
    bup[...] = jnp.sum(dot(split3(bup0[...]), perm[...]), axis=0, keepdims=True)

    eye = (
        lax.broadcasted_iota(jnp.int32, (COLS, COLS), 0)
        == lax.broadcasted_iota(jnp.int32, (COLS, COLS), 1)
    ).astype(F32)

    def mask_row(j, total):
        cells = pl.ds(pl.multiple_of(j * COLS, COLS), COLS)
        sea = jnp.sum(eye * oc[pl.ds(j, 1), :].astype(F32), axis=1, keepdims=True)
        value = cs[j].astype(F32) * sea
        masked[cells, :] = value
        value = value * scale[...]
        dbr[cells, :] = value.astype(BF16)
        return total + sub8(value)

    g_bdown = lax.fori_loop(0, ROWS, mask_row, jnp.zeros((8, CH), F32))
    dhid[...] = dot(dbr[...], wdown[...])

    finish_rows(first)
    second = corners(hv, cw, ce, qs, qr)
    for copy in first[2:]:
        copy.wait()
    for copy in second:
        copy.wait()
    widen(wide, hv, xs, hw, he, cw, ce)

    def put_conv(ct, lanes, total):
        for j in range(ROWS):
            conv[j * COLS : (j + 1) * COLS, lanes] = total[j]

    conv_into(wide, taps, False, put_conv)

    def norm_row(j, _):
        cells = pl.ds(pl.multiple_of(j * COLS, COLS), COLS)
        value = conv[cells, :]
        value = value - jnp.mean(value, axis=1, keepdims=True)
        r = lax.rsqrt(jnp.mean(value * value, axis=1, keepdims=True) + 1e-06)
        value = value * r
        rstd[cells, :] = r
        unit[cells, :] = value
        normed[cells, :] = (value * gain[...] + shift[...]).astype(BF16)
        return 0

    lax.fori_loop(0, ROWS, norm_row, 0)
    pre[...] = dot(normed[...], wup[...])

    def gelu_row(j, totals):
        cells = pl.ds(pl.multiple_of(j * COLS, COLS), COLS)
        done = []
        for k in range(3):
            lanes = slice(k * 256, k * 256 + 256)
            v = pre[cells, lanes] + bup[:, lanes]
            square = v * v
            tanh = jnp.tanh(v * (COEFF + COEFF * CUBIC * square))
            half = 0.5 + 0.5 * tanh
            value = v * half
            slope = half + value * (1.0 - tanh) * (COEFF + 3.0 * CUBIC * COEFF * square)
            hidden[cells, lanes] = value.astype(BF16)
            grad = dhid[cells, lanes] * slope
            dpre[cells, lanes] = grad.astype(BF16)
            done.append(totals[k] + sub8(grad))
        return tuple(done)

    g_bup = lax.fori_loop(
        0, ROWS, gelu_row, tuple(jnp.zeros((8, 256), F32) for _ in range(3))
    )
    g_bup = jnp.concatenate([jnp.sum(v, axis=0, keepdims=True) for v in g_bup], axis=1)

    dnorm[...] = dot(dpre[...], wup[...], (1, 1))

    def back_row(j, totals):
        cells = pl.ds(pl.multiple_of(j * COLS, COLS), COLS)
        u = unit[cells, :]
        grad = dnorm[cells, :]
        product = grad * u
        scaled = grad * gain[...]
        mean_a = jnp.mean(scaled, axis=1, keepdims=True)
        mean_b = jnp.mean(product * gain[...], axis=1, keepdims=True)
        value = (rstd[cells, :] * (scaled - mean_a - u * mean_b)).astype(BF16)
        dcb[j] = value
        value = value.astype(F32)
        for ct in range(3):
            dcv[ct, j] = value[:, ct * 128 : ct * 128 + 128]
        return totals[0] + sub8(product), totals[1] + sub8(grad)

    zero = jnp.zeros((8, CH), F32)
    g_gain, g_shift = lax.fori_loop(0, ROWS, back_row, (zero, zero))

    @pl.when(top)
    def _():
        dv[1] = jnp.zeros((PAD, COLS, CH), BF16)

    @pl.when(bottom)
    def _():
        dv[0] = jnp.zeros((PAD, COLS, CH), BF16)

    third = halo(dcb, dw, de, dv, ds, dr)

    for half in range(2):
        units = slice(half * 384, half * 384 + 384)
        g[0, half] = dot(dpre[:, units], normed[...], (0, 0)).astype(BF16)
        g[1, half] = dot(dbr[...], hidden[:, units], (0, 0)).astype(BF16)
    cross = remote(g.at[:, 1 - c], gc, cs_s.at[0], cs_r.at[0], other)
    cross.start()

    branch = dot(hidden[...], wdown[...], (1, 1)) + bdown[...]
    g_scale = jnp.sum(masked[...] * branch, axis=0, keepdims=True)
    back = jnp.sum(dot(split3(g_bup), perm[...], (1, 1)), axis=0, keepdims=True)
    s[...] = jnp.zeros((64, 512), F32)
    s[49:50, 0:CH] = jnp.sum(g_gain, axis=0, keepdims=True)
    s[50:51, 0:CH] = jnp.sum(g_shift, axis=0, keepdims=True)
    s[51:52, 0:CH] = jnp.sum(g_bdown, axis=0, keepdims=True)
    s[52:53, 0:CH] = g_scale
    s[53:54, 0:CH] = back[:, 0:CH]
    s[54:55, 0:CH] = back[:, CH:HID]

    def tap_tile(ct, _):
        lanes = pl.ds(pl.multiple_of(ct * 128, 128), 128)
        for b in range(KW):
            total = [jnp.zeros((8, 128), F32) for _ in range(KW)]
            for r in range(ROWS + 2 * PAD):
                value = wide[ct, r, 5 + b : 5 + b + COLS, :]
                for a in range(KW):
                    j = r - a
                    if 0 <= j < ROWS:
                        total[a] = total[a] + sub8(value * dcv[ct, j])
            for a in range(KW):
                s[a * KW + b : a * KW + b + 1, lanes] = jnp.sum(total[a], axis=0, keepdims=True)
        return 0

    lax.fori_loop(0, 3, tap_tile, 0)

    half_s = pl.multiple_of((1 - c) * 32, 32)
    cross_s = remote(s.at[pl.ds(half_s, 32)], sc, sa_s.at[0], sa_r.at[0], other)
    cross_s.start()

    finish_rows(third)
    fourth = corners(dv, ew, ee, es, er)

    cross.wait()
    for k in range(2):
        for q in range(4):
            rows = slice(q * 96, q * 96 + 96)
            h[k, q] = (g[k, c, rows, :].astype(F32) + gc[k, rows, :].astype(F32)).astype(BF16)
    along = []
    for d in range(1, 4):
        up = remote(h.at[0, lax.rem(x + d, 4)], h1.at[0, d - 1], f_s.at[0, d - 1], f_r.at[0, d - 1], peer_x(d))
        down = remote(h.at[1, lax.rem(y + d, 4)], h1.at[1, d - 1], f_s.at[1, d - 1], f_r.at[1, d - 1], peer_y(d))
        up.start()
        down.start()
        along += [up, down]

    cross_s.wait()
    mine_s = pl.multiple_of(c * 32, 32)
    s1[...] = (s[pl.ds(mine_s, 32), :] + sc[...]).reshape(4, 8, 512)
    small = []
    for d in range(1, 4):
        copy = remote(s1.at[lax.rem(x + d, 4)], sx.at[d - 1], sx_s.at[d - 1], sx_r.at[d - 1], peer_x(d))
        copy.start()
        small.append(copy)

    for copy in third[2:]:
        copy.wait()
    for copy in fourth:
        copy.wait()
    widen(dwide, dv, dcb, dw, de, ew, ee)

    def put_back(ct, lanes, total):
        for j in range(ROWS):
            value = cs[j, :, lanes].astype(F32) + total[j]
            gs_out[j, :, lanes] = value.astype(BF16)
            if 4 <= j < 7:
                edge_out[j - 4, :, lanes] = value

    conv_into(dwide, taps, True, put_back)

    def put_beyond(lanes, total):
        for j in range(PAD):
            beyond_out[j, :, lanes] = total[j].astype(BF16)

    beyond_into(dwide, taps, put_beyond)

    for copy in small:
        copy.wait()
    s2[...] = s1[x] + sx[0] + sx[1] + sx[2]
    small = []
    for d in range(1, 4):
        chunk = pl.ds(pl.multiple_of(lax.rem(y + d, 4) * 128, 128), 128)
        copy = remote(s2.at[:, chunk], sy.at[d - 1], sy_s.at[d - 1], sy_r.at[d - 1], peer_y(d))
        copy.start()
        small.append(copy)

    for copy in along:
        copy.wait()
    spread = onehot(CH, 512, lambda p: jnp.where(p % 128 < 96, p // 128 * 96 + p % 128, -1))
    for k in range(2):
        mine = h[k, (x, y)[k]].astype(F32)
        mine = mine + h1[k, 0].astype(F32) + h1[k, 1].astype(F32) + h1[k, 2].astype(F32)
        mine = dot(mine.astype(BF16), spread).astype(BF16)
        for q in range(4):
            h2[k, q] = mine[:, q * 128 : q * 128 + 128]
    along = []
    for d in range(1, 4):
        up = remote(h2.at[0, lax.rem(y + d, 4)], r2.at[0, d - 1], k_s.at[0, d - 1], k_r.at[0, d - 1], peer_y(d))
        down = remote(h2.at[1, lax.rem(x + d, 4)], r2.at[1, d - 1], k_s.at[1, d - 1], k_r.at[1, d - 1], peer_x(d))
        up.start()
        down.start()
        along += [up, down]

    for copy in small:
        copy.wait()
    mine_y = pl.ds(pl.multiple_of(y * 128, 128), 128)
    s3[...] = s2[:, mine_y] + sy[0] + sy[1] + sy[2]
    small = []
    for d in range(1, 16):
        copy = remote(s3, sz.at[z], sz_s.at[d - 1], sz_r.at[d - 1], peer_z(d))
        copy.start()
        small.append(copy)

    for copy in along:
        copy.wait()
    parts = []
    for k in range(2):
        mine = h2[k, (y, x)[k]].astype(F32)
        mine = mine + r2[k, 0].astype(F32) + r2[k, 1].astype(F32) + r2[k, 2].astype(F32)
        parts.append(mine.astype(BF16))
    pick_up = onehot(128, 256, lambda p: jnp.where(p % 128 < 48, p // 128 * 48 + p % 128, -1))
    pick_down = onehot(
        96, 256, lambda p: jnp.where((p % 128 >= 64) & (p % 128 < 112), p // 128 * 48 + p % 128 - 64, -1)
    )
    both = dot(parts[0], pick_up) + dot(parts[1], pick_down, (0, 0))[0:96]
    rows_to = onehot(96, 128, lambda p: jnp.where(p % 16 < 12, p // 16 * 12 + p % 16, -1))
    tiles = dot(rows_to, both.astype(BF16), (0, 0)).astype(BF16)
    for q in range(16):
        t[q] = tiles[q % 8 * 16 : q % 8 * 16 + 16, q // 8 * 128 : q // 8 * 128 + 128]
    along = []
    for d in range(1, 16):
        copy = remote(t.at[lax.rem(z + d, 16)], tz.at[d - 1], z_s.at[d - 1], z_r.at[d - 1], peer_z(d))
        copy.start()
        along.append(copy)

    sz[z] = s3[...]
    for copy in small:
        copy.wait()
    total = sz[0]
    for q in range(1, 16):
        total = total + sz[q]
    b1[:, mine_y] = total * FACTOR
    gather = []
    for d in range(1, 4):
        copy = remote(b1.at[:, mine_y], b1.at[:, mine_y], gy_s.at[d - 1], gy_r.at[d - 1], peer_y(d))
        copy.start()
        gather.append(copy)
    for copy in gather:
        copy.wait()
    b2[x] = b1[...]
    gather = []
    for d in range(1, 4):
        copy = remote(b1, b2.at[x], gx_s.at[d - 1], gx_r.at[d - 1], peer_x(d))
        copy.start()
        gather.append(copy)
    for copy in gather:
        copy.wait()
    b3[c] = b2[...]
    copy = remote(b2, b3.at[c], gc_s.at[0], gc_r.at[0], other)
    copy.start()
    copy.wait()
    final = b3[...].reshape(64, 512)
    gk_out[...] = final[0:49, 0:CH]
    gc_out[...] = final[49:53, 0:CH]
    gb_out[...] = final[53:55, 0:CH]

    for copy in along:
        copy.wait()
    total = t[z].astype(F32)
    for d in range(15):
        total = total + tz[d].astype(F32)
    tile_out[...] = total * FACTOR


def fused(state, ghost, cot, ocean, taps, gain, shift, wup, bup, wdown, bdown, scale):
    sds = jax.ShapeDtypeStruct
    vm = pltpu.VMEM
    dma = pltpu.SemaphoreType.DMA
    any_spec = pl.BlockSpec(memory_space=pl.ANY)
    vm_spec = pl.BlockSpec(memory_space=pltpu.VMEM)
    edge16 = (ROWS, 16, CH)
    corner = (2, PAD, 16, CH)
    scratch = [
        vm((ROWS, COLS, CH), BF16), vm((ROWS, COLS, CH), BF16), vm((ROWS, COLS), jnp.int32),
        vm((49, CH), F32), vm((1, CH), F32), vm((1, CH), F32), vm((CH, HID), BF16), vm((1, HID), F32),
        vm((CH, HID), BF16), vm((1, CH), F32), vm((1, CH), F32),
        vm(edge16, BF16), vm(edge16, BF16), vm((2, PAD, COLS, CH), BF16), vm(corner, BF16), vm(corner, BF16),
        vm(edge16, BF16), vm(edge16, BF16), vm((2, PAD, COLS, CH), BF16), vm(corner, BF16), vm(corner, BF16),
        vm((3, 14, WIDE, 128), F32), vm((3, 14, WIDE, 128), F32),
        vm((CH, HID), BF16), vm((CH, HID), BF16), vm((1, HID), F32),
        vm((CELLS, CH), F32), vm((CELLS, CH), F32), vm((CELLS, 1), F32), vm((CELLS, CH), BF16),
        vm((CELLS, CH), F32), vm((CELLS, CH), BF16), vm((CELLS, HID), F32), vm((CELLS, HID), F32),
        vm((CELLS, HID), BF16), vm((CELLS, HID), BF16), vm((CELLS, CH), F32),
        vm((3, ROWS, COLS, 128), F32), vm((ROWS, COLS, CH), BF16),
        vm((2, 2, 384, 384), BF16), vm((2, 384, 384), BF16), vm((2, 4, 96, 384), BF16),
        vm((2, 3, 96, 384), BF16), vm((2, 4, 96, 128), BF16), vm((2, 3, 96, 128), BF16),
        vm((16, 16, 128), BF16), vm((15, 16, 128), BF16), vm((HID, HID), BF16),
        vm((64, 512), F32), vm((32, 512), F32), vm((4, 8, 512), F32), vm((3, 8, 512), F32), vm((8, 512), F32),
        vm((3, 8, 128), F32), vm((8, 128), F32), vm((16, 8, 128), F32), vm((8, 512), F32), vm((4, 8, 512), F32),
        vm((2, 4, 8, 512), F32),
        dma((12,)), dma((4,)), dma((4,)), dma((2,)), dma((2,)), dma((4,)), dma((4,)), dma((2,)), dma((2,)),
        dma((1,)), dma((1,)), dma((2, 3)), dma((2, 3)), dma((2, 3)), dma((2, 3)), dma((15,)), dma((15,)),
        dma((1,)), dma((1,)), dma((3,)), dma((3,)), dma((3,)), dma((3,)), dma((15,)), dma((15,)),
        dma((3,)), dma((3,)), dma((3,)), dma((3,)), dma((1,)), dma((1,)),
    ]
    return pl.pallas_call(
        body,
        out_shape=[
            sds((ROWS, COLS, CH), BF16), sds((PAD, COLS, CH), F32), sds((PAD, COLS, CH), BF16),
            sds((16, 128), F32), sds((49, CH), F32), sds((4, CH), F32), sds((2, CH), F32),
        ],
        in_specs=[any_spec] * 12,
        out_specs=[vm_spec] * 7,
        scratch_shapes=scratch,
        compiler_params=pltpu.CompilerParams(
            collective_id=0, has_side_effects=True, vmem_limit_bytes=50 * 2**20
        ),
        name="block",
    )(state, ghost, cot, ocean, taps, gain, shift, wup, bup, wdown, bdown, scale)


def across(strip, partner):
    pivot = lax.rem(partner + lax.axis_index("ia"), LANES)

    def branch(k):
        pairs = [
            (a * BANDS + BANDS - 1, (k - a) % LANES * BANDS + BANDS - 1) for a in range(LANES)
        ]
        return lambda v: lax.ppermute(v, ("ia", "ja"), pairs)

    return lax.switch(pivot, [branch(k) for k in range(LANES)], strip)[::-1, ::-1]


def local(
    state, cotangent, ocean, fold_partner, kernel, ln_gain, ln_shift, w_up, b_up, w_down, b_down, layer_scale
):
    on_top = lax.axis_index("ja") == BANDS - 1
    ghost = across(state[4:7], fold_partner[0])
    gs, edge, beyond, tile, g_kernel, g_chan, g_bup = fused(
        state, ghost, cotangent, ocean, kernel, ln_gain[None], ln_shift[None], w_up, b_up[None],
        w_down, b_down[None], layer_scale[None],
    )
    fold = across(beyond, fold_partner[0])
    edge = edge + jnp.where(on_top, fold.astype(F32), 0.0)
    grad_state = jnp.concatenate([gs[0:4], edge.astype(BF16), gs[7:8]], axis=0)
    grad_up = tile[0:12, 0:48].T
    grad_down = tile[0:12, 64:112].T
    return grad_state, grad_up, grad_down, g_kernel, g_chan, g_bup.reshape(HID)


def solution(mesh):
    placed = (P("ja", "ia", None), P("ja", "ia", None), P("ja", "ia"), P("ia")) + (P(),) * 8
    return jax.shard_map(
        local,
        mesh=mesh,
        in_specs=placed,
        out_specs=(P("ja", "ia", None), P("ja", "ia"), P("ja", "ia"), P(), P(), P()),
        check_vma=False,
    )
```

time: 1090 us -> 170 us (0.16)
  the two profiles are of different devices: /device:TPU:1 before, /device:TPU:409 now
where the time goes in v1:
time: 170 us; the launch traced here: 169 us
  Pallas kernels  94 us (55%)
  starting transfers between devices  36.7 us (22%)
  waiting for transfers between devices  23.8 us (14%)
  local copies, waits for them, and re-layouts  12.3 us (7%)
    pallas_call x1, Pallas kernels, fused(): pl.pallas_call(body, out_shape=[sds((ROWS, COLS, CH), BF16), sds((PAD, CO...  94 us
    ppermute x2, starting transfers between devices, branch(): return lambda v: lax.ppermute(v, ('ia', 'ja'), pairs)  36.7 us
    ppermute x2, waiting for transfers between devices, branch(): return lambda v: lax.ppermute(v, ('ia', 'ja'), pairs)  23.8 us
    unnamed x24, local copies, waits for them, and re-layouts  6.96 us
  transfers between devices with their start and end apart: 2, of which 2 were waited for; matrix products, arithmetic and copies ran while one was open for 0% of the time, Pallas kernels for 0%

profile of v1, /device:TPU:409, one launch (start us, length us, event | category | flops | bytes accessed | tf_op | source)
XLA Modules:
  0.0 169.0 jit_solution(1361249071786636746)
XLA Ops:
  1.3 0.0 copy-start.7
  1.3 0.7 copy-done.7
  2.0 0.0 copy-start.8
  2.0 0.7 copy-done.8
  2.7 0.0 copy-start.9
  2.7 0.0 copy-start.10
  2.7 0.7 copy-done.9
  3.3 0.0 copy-start.6
  3.3 0.0 copy-done.10
  3.4 0.7 copy-done.6
  4.0 0.0 copy-start.2
  4.0 0.0 copy-start.3
  4.0 1.0 slice.207
  5.0 30.5 %conditional.2 = (bf16[3,32,384]{2,1,0:T(8,128)(2,1)}) conditional(s32[]{:T(128)} %clamp.4, bf16[3,32,384]{2,1,0:T(8,128)(2,1)S(1)} %slice.207, bf16[3,32,384]{2,1,0:T(8,128)(2,1)S(1)} %slice.207, bf16[3,32,384]{2,1,0:T(8,128)(2,1)S(1)} %slice.207, bf16[3,32,384]{2,1,0:T(8,128)(2,1)S(1)} %slice.207, ...), branch_computations={%region_0.0_spmd, %region_1.0_spmd, %region_2.0_spmd, %region_3.0_... | conditional | bytes 294960 | solution.py:579
  5.0 18.6 %collective-permute-start.47 = (bf16[3,32,384]{2,1,0:T(8,128)(2,1)S(1)}, bf16[3,32,384]{2,1,0:T(8,128)(2,1)}, u32[]{:S(2)}, u32[]{:S(2)}) collective-permute-start(bf16[3,32,384]{2,1,0:T(8,128)(2,1)S(1)} %param.47), channel_id=1, source_target_pairs={{7,383},{15,375},{23,367},{31,359},{39,351},{47,343},{55,335},{63,... | collective-permute-start | bytes 221192 | tf_op jit(solution)/shard_map/cond/branch_47_fun/ppermute | solution.py:577
  23.6 11.9 %collective-permute-done.47 = bf16[3,32,384]{2,1,0:T(8,128)(2,1)} collective-permute-done((bf16[3,32,384]{2,1,0:T(8,128)(2,1)S(1)}, bf16[3,32,384]{2,1,0:T(8,128)(2,1)}, u32[]{:S(2)}, u32[]{:S(2)}) %collective-permute-start.47) | collective-permute-done | bytes 73760 | tf_op jit(solution)/shard_map/cond/branch_47_fun/ppermute | solution.py:577
  35.5 0.0 copy-start.5
  35.5 1.5 rev.6.ghost
  37.0 0.0 copy-done.2
  37.0 0.0 copy-done.3
  37.0 0.0 copy-done.5
  37.0 0.0 copy-start
  37.1 1.1 copy-done
  38.1 0.0 copy-start.1
  38.1 1.1 copy-done.1
  39.2 0.0 copy-start.4
  39.2 0.9 copy-done.4
  40.1 94.0 %block.1 = (bf16[8,32,384]{2,1,0:T(8,128)(2,1)S(1)}, f32[3,32,384]{2,1,0:T(8,128)S(1)}, bf16[3,32,384]{2,1,0:T(8,128)(2,1)S(1)}, f32[16,128]{1,0:T(8,128)S(1)}, ...) custom-call(bf16[8,32,384]{2,1,0:T(8,128)(2,1)S(1)} %copy-done.2, ...), custom_call_target="tpu_custom_call" | custom-call | tf_op jit(solution)/shard_map/block/pallas_call | solution.py:554
  134.1 0.6 reshape.15
  134.7 0.7 slice_bitcast_fusion
  135.4 30.2 %conditional.3 = (bf16[3,32,384]{2,1,0:T(8,128)(2,1)}) conditional(s32[]{:T(128)} %clamp.4, bf16[3,32,384]{2,1,0:T(8,128)(2,1)S(1)} %get-tuple-element.273, bf16[3,32,384]{2,1,0:T(8,128)(2,1)S(1)} %get-tuple-element.273, bf16[3,32,384]{2,1,0:T(8,128)(2,1)S(1)} %get-tuple-element.273, ...), branch_computations={%region_64.0_spmd, %region_65.0_spmd, %region_66.0_spmd, %region_6... | conditional | bytes 294960 | solution.py:579
  135.4 18.2 %collective-permute-start.111 = (bf16[3,32,384]{2,1,0:T(8,128)(2,1)S(1)}, bf16[3,32,384]{2,1,0:T(8,128)(2,1)}, u32[]{:S(2)}, u32[]{:S(2)}) collective-permute-start(bf16[3,32,384]{2,1,0:T(8,128)(2,1)S(1)} %param.111), channel_id=1, source_target_pairs={{7,383},{15,375},{23,367},{31,359},{39,351},{47,343},{55,335},{63,... | collective-permute-start | bytes 221192 | tf_op jit(solution)/shard_map/cond/branch_47_fun/ppermute | solution.py:577
  153.6 11.9 %collective-permute-done.111 = bf16[3,32,384]{2,1,0:T(8,128)(2,1)} collective-permute-done((bf16[3,32,384]{2,1,0:T(8,128)(2,1)S(1)}, bf16[3,32,384]{2,1,0:T(8,128)(2,1)}, u32[]{:S(2)}, u32[]{:S(2)}) %collective-permute-start.111) | collective-permute-done | bytes 73760 | tf_op jit(solution)/shard_map/cond/branch_47_fun/ppermute | solution.py:577
  165.5 1.5 rev.7
  167.1 0.7 pad_maximum_fusion
  167.8 0.6 copy.149
  168.4 0.6 copy.150
  (8 shorter events, 0.1 us)
Async XLA Ops:
  1.3 0.7 copy-start.7
  2.0 0.7 copy-start.8
  2.7 0.7 copy-start.9
  2.7 0.7 copy-start.10
  3.3 0.7 copy-start.6
  4.0 33.0 %copy-start.2 = (bf16[8,32,384]{2,1,0:T(8,128)(2,1)S(1)}, bf16[8,32,384]{2,1,0:T(8,128)(2,1)}, u32[]{:S(2)}) copy-start(bf16[8,32,384]{2,1,0:T(8,128)(2,1)} %state.1) | copy-start | bytes 589828
  4.0 33.0 %copy-start.3 = (bf16[8,32,384]{2,1,0:T(8,128)(2,1)S(1)}, bf16[8,32,384]{2,1,0:T(8,128)(2,1)}, u32[]{:S(2)}) copy-start(bf16[8,32,384]{2,1,0:T(8,128)(2,1)} %cot.1) | copy-start | bytes 589828
  5.0 30.5 %collective-permute-start.47 = (bf16[3,32,384]{2,1,0:T(8,128)(2,1)S(1)}, bf16[3,32,384]{2,1,0:T(8,128)(2,1)}, u32[]{:S(2)}, u32[]{:S(2)}) collective-permute-start(bf16[3,32,384]{2,1,0:T(8,128)(2,1)S(1)} %param.47), channel_id=1, source_target_pairs={{7,383},{15,375},{23,367},{31,359},{39,351},{47,343},{55,335},{63,... | collective-permute-start | bytes 221192 | tf_op jit(solution)/shard_map/cond/branch_47_fun/ppermute | solution.py:577
  35.5 1.6 copy-start.5
  37.0 1.1 copy-start
  38.1 1.1 copy-start.1
  39.2 0.9 copy-start.4
  135.4 30.1 %collective-permute-start.111 = (bf16[3,32,384]{2,1,0:T(8,128)(2,1)S(1)}, bf16[3,32,384]{2,1,0:T(8,128)(2,1)}, u32[]{:S(2)}, u32[]{:S(2)}) collective-permute-start(bf16[3,32,384]{2,1,0:T(8,128)(2,1)S(1)} %param.111), channel_id=1, source_target_pairs={{7,383},{15,375},{23,367},{31,359},{39,351},{47,343},{55,335},{63,... | collective-permute-start | bytes 221192 | tf_op jit(solution)/shard_map/cond/branch_47_fun/ppermute | solution.py:577

commit v2 on v1

v2 whole, which is shorter than its diff:
```python
import functools
import math

import jax
import jax.numpy as jnp
from jax import lax
from jax.experimental import pallas as pl
from jax.experimental.pallas import tpu as pltpu
from jax.sharding import PartitionSpec as P

KW = 7
PAD = 3
ROWS = 8
COLS = 32
CH = 384
HID = 768
CELLS = ROWS * COLS
WIDE = 48
F32 = jnp.float32
BF16 = jnp.bfloat16
LANES = 64
BANDS = 8
COEFF = 0.7978845608028654
CUBIC = 0.044715
FACTOR = 1.0 / math.sqrt(ROWS * BANDS * COLS * LANES)


def place(x, y, z, c):
    return {"ia": x * 16 + lax.rem(z, 8) * 2 + c, "ja": y * 2 + z // 8}


def dot(a, b, dims=(1, 0)):
    return lax.dot_general(
        a, b, (((dims[0],), (dims[1],)), ((), ())), preferred_element_type=F32
    )


def sub8(v):
    return v[0:8] + v[8:16] + v[16:24] + v[24:32]


def onehot(rows, cols, target):
    want = target(lax.broadcasted_iota(jnp.int32, (1, cols), 1))
    here = lax.broadcasted_iota(jnp.int32, (rows, cols), 0)
    return jnp.where(here == want, 1.0, 0.0).astype(BF16)


def split3(v):
    hi = v.astype(BF16)
    rest = v - hi.astype(F32)
    mid = rest.astype(BF16)
    low = (rest - mid.astype(F32)).astype(BF16)
    zeros = jnp.zeros((13, v.shape[1]), F32)
    return jnp.concatenate(
        [hi.astype(F32), mid.astype(F32), low.astype(F32), zeros], axis=0
    ).astype(BF16)


def conv_part(wide, taps, flip, rows, spans, read, write):
    def tile(ct, _):
        lanes = pl.ds(pl.multiple_of(ct * 128, 128), 128)
        for start, width in spans:
            hit = [j for j in range(ROWS) if any(0 <= r - j < KW for r in rows)]
            total = {j: read(ct, j, start, width) for j in hit}
            for b in range(KW):
                weight = []
                for a in range(KW):
                    tap = a * KW + b
                    tap = KW * KW - 1 - tap if flip else tap
                    weight.append(taps[tap : tap + 1, lanes])
                for r in rows:
                    value = wide[ct, r, 5 + b + start : 5 + b + start + width, :]
                    for a in range(KW):
                        if r - a in total:
                            total[r - a] = total[r - a] + value * weight[a]
            for j in hit:
                write(ct, lanes, j, start, width, total[j])
        return 0

    lax.fori_loop(0, 3, tile, 0)


def fold_into(edge, taps, read, write):
    def tile(ct, _):
        lanes = pl.ds(pl.multiple_of(ct * 128, 128), 128)
        total = [read(j, lanes) for j in range(3)]
        for b in range(KW):
            for j in range(3):
                for e in range(j + 1):
                    a = e + 6 - j
                    weight = taps[a * KW + b : a * KW + b + 1, lanes]
                    total[j] = total[j] + edge[ct, e, 5 + b : 5 + b + COLS, :] * weight
        for j in range(3):
            write(j, lanes, total[j])
        return 0

    lax.fori_loop(0, 3, tile, 0)


def fold_slots(p):
    q = jnp.where(p < 112, p - 96, p - 112)
    first = q // 3 * COLS + q % 3
    edge = jnp.where(q < 9, jnp.where(p < 112, first, first + COLS - 3), -1)
    return jnp.where(p < 96, p, edge)


def fold_cells(p):
    row, col = p // WIDE, p % WIDE
    west = 96 + (2 - row) * 3 + 7 - col
    east = 112 + (2 - row) * 3 + 42 - col
    inner = 95 - row * COLS - (col - 8)
    slot = jnp.where(col < 8, west, jnp.where(col < 40, inner, east))
    return jnp.where((col >= 5) & (col < 43), slot, -1)


def fold_swap(p):
    return p % 16 // 2 * 16 + p // 16 * 2 + p % 2


def body(
    state, cot, ocean, partner, taps_in, gain_in, shift_in, wup_in, bup_in, wdown_in, bdown_in, scale_in,
    gs_out, tile_out, small_out,
    xs, cs, oc, part, taps, gain, shift, wup0, bup0, wdown0, bdown, scale,
    hw, he, hv, cw, ce, dw, de, dv, ew, ee,
    wide, dwide, edge, acc, bacc, edge_rows, wup, wdown, bup,
    unit, rstd, normed, masked, dbr, dhid, pre, hidden, dpre, dnorm, dcv, dcb,
    g, gc, h, h1, h2, r2, t, tz, perm,
    s, sc, s1, sx, s2, sy, s3, sz, b1, b2, b3, fold,
    loc, hs, hr, qs, qr, ds, dr, es, er, cs_s, cs_r, f_s, f_r, k_s, k_r, z_s, z_r,
    sa_s, sa_r, sx_s, sx_r, sy_s, sy_r, sz_s, sz_r, gy_s, gy_r, gx_s, gx_r, gc_s, gc_r, fold_s, fold_r,
):
    ia, ja = lax.axis_index("ia"), lax.axis_index("ja")
    x, zl, c = ia // 16, lax.rem(ia // 2, 8), lax.rem(ia, 2)
    y, zh = ja // 2, lax.rem(ja, 2)
    z = zh * 8 + zl
    u = x * 2 + c
    top, bottom = ja == BANDS - 1, ja == 0
    east = {"ia": lax.rem(ia + 1, LANES), "ja": ja}
    west = {"ia": lax.rem(ia + LANES - 1, LANES), "ja": ja}
    north = {"ia": ia, "ja": ja + 1}
    south = {"ia": ia, "ja": ja - 1}

    def remote(src, dst, send, recv, device):
        return pltpu.make_async_remote_copy(
            src_ref=src, dst_ref=dst, send_sem=send, recv_sem=recv,
            device_id=device, device_id_type=pl.DeviceIdType.MESH,
        )

    def peer_x(d):
        return place(lax.rem(x + d, 4), y, z, c)

    def peer_y(d):
        return place(x, lax.rem(y + d, 4), z, c)

    def peer_z(d):
        return place(x, y, lax.rem(z + d, 16), c)

    def peer_u(d):
        to = lax.rem(u + d, 8)
        return {"ia": to // 2 * 16 + zl * 2 + lax.rem(to, 2), "ja": ja}

    def peer_v(d):
        return {"ia": x * 16 + lax.rem(zl + d, 8) * 2 + c, "ja": ja}

    other = place(x, y, z, 1 - c)

    loads = [
        pltpu.make_async_copy(src, dst, loc.at[i])
        for i, (src, dst) in enumerate(
            [
                (state, xs), (cot, cs), (ocean, oc), (taps_in, taps), (gain_in, gain), (shift_in, shift),
                (wup_in, wup0), (bup_in, bup0), (wdown_in, wdown0), (bdown_in, bdown), (scale_in, scale),
                (partner, part),
            ]
        )
    ]
    for load in loads:
        load.start()

    barrier = pltpu.get_barrier_semaphore()

    def greet(device):
        pl.semaphore_signal(barrier, inc=1, device_id=device, device_id_type=pl.DeviceIdType.MESH)

    greet({"ia": ia, "ja": lax.rem(ja + 1, BANDS)})
    greet({"ia": ia, "ja": lax.rem(ja + BANDS - 1, BANDS)})
    greet(east)
    greet(west)

    @pl.when(top)
    def _():
        for d in range(1, 8):
            greet(peer_u(d))
            greet(peer_v(d))

    for d in range(1, 16):
        greet(peer_z(d))
    for d in range(1, 4):
        greet(peer_x(d))
        greet(peer_y(d))
    greet(other)

    for load in loads:
        load.wait()

    def old(p):
        return (p % 384) // 96 * 192 + (p % 96) // 12 * 24 + p // 384 * 12 + p % 12

    perm[...] = onehot(HID, HID, old)
    wup[...] = dot(wup0[...], perm[...]).astype(BF16)
    wdown[...] = dot(wdown0[...], perm[...]).astype(BF16)
    bup[...] = jnp.sum(dot(split3(bup0[...][None]), perm[...]), axis=0, keepdims=True)

    eye = (
        lax.broadcasted_iota(jnp.int32, (COLS, COLS), 0)
        == lax.broadcasted_iota(jnp.int32, (COLS, COLS), 1)
    ).astype(F32)

    def mask_row(j, total):
        sea = jnp.sum(eye * oc[pl.ds(j, 1), :].astype(F32), axis=1, keepdims=True)
        value = cs[j].astype(F32) * sea
        halves = (value[8:24], jnp.concatenate([value[0:8], value[24:32]], axis=0))
        for k in range(2):
            cells = pl.ds(pl.multiple_of(k * 128 + j * 16, 16), 16)
            masked[cells, :] = halves[k]
            dbr[cells, :] = (halves[k] * scale[...][None]).astype(BF16)
        return total + sub8(value * scale[...][None])

    g_bdown = lax.fori_loop(0, ROWS, mask_row, jnp.zeros((8, CH), F32))
    dhid[...] = dot(dbr[...], wdown[...])

    def widen_own(dst, centre):
        for ct in range(3):
            lanes = slice(ct * 128, ct * 128 + 128)
            for r in range(ROWS):
                dst[ct, PAD + r, 8:40, :] = centre[r, :, lanes].astype(F32)

    def widen_sides(dst, w, e):
        for ct in range(3):
            lanes = slice(ct * 128, ct * 128 + 128)
            for r in range(ROWS):
                dst[ct, PAD + r, 0:8, :] = w[r, :, lanes].astype(F32)[8:16]
                dst[ct, PAD + r, 40:48, :] = e[r, :, lanes].astype(F32)[0:8]

    def widen_rows(dst, v, k):
        for ct in range(3):
            lanes = slice(ct * 128, ct * 128 + 128)
            for q in range(PAD):
                dst[ct, q + k * (ROWS + PAD), 8:40, :] = v[k, q, :, lanes].astype(F32)

    def widen_corners(dst, w, e, k):
        for ct in range(3):
            lanes = slice(ct * 128, ct * 128 + 128)
            for q in range(PAD):
                dst[ct, q + k * (ROWS + PAD), 0:8, :] = w[k, q, :, lanes].astype(F32)[8:16]
                dst[ct, q + k * (ROWS + PAD), 40:48, :] = e[k, q, :, lanes].astype(F32)[0:8]

    widen_own(wide, xs)

    pl.semaphore_wait(barrier, 26 + jnp.where(top, 14, 0))

    def halo(src, w, e, v, send, recv):
        to_north = remote(src.at[5:8], v.at[0], send.at[0], recv.at[0], north)
        to_south = remote(src.at[0:3], v.at[1], send.at[1], recv.at[1], south)
        to_east = remote(src.at[:, 16:32], w, send.at[2], recv.at[2], east)
        to_west = remote(src.at[:, 0:16], e, send.at[3], recv.at[3], west)

        @pl.when(jnp.logical_not(top))
        def _():
            to_north.start()

        @pl.when(jnp.logical_not(bottom))
        def _():
            to_south.start()

        to_east.start()
        to_west.start()
        return to_north, to_south, to_east, to_west

    def finish_rows(copies):
        to_north, to_south, _, _ = copies

        @pl.when(jnp.logical_not(top))
        def _():
            to_north.wait_send()
            to_south.wait_recv()

        @pl.when(jnp.logical_not(bottom))
        def _():
            to_south.wait_send()
            to_north.wait_recv()

    def corners(v, w, e, send, recv):
        copies = []
        for k in range(2):
            copies.append(remote(v.at[k, :, 16:32], w.at[k], send.at[2 * k], recv.at[2 * k], east))
            copies.append(remote(v.at[k, :, 0:16], e.at[k], send.at[2 * k + 1], recv.at[2 * k + 1], west))
        copies[0].start()
        copies[1].start()

        @pl.when(jnp.logical_not(top))
        def _():
            copies[2].start()
            copies[3].start()

        return copies

    def finish_corners(dst, copies, w, e):
        copies[0].wait()
        copies[1].wait()
        widen_corners(dst, w, e, 0)

        @pl.when(jnp.logical_not(top))
        def _():
            copies[2].wait()
            copies[3].wait()
            widen_corners(dst, w, e, 1)

    def fold_copies(k, step, peer, me):
        return [
            remote(
                fold.at[k, step, 0, lax.rem(me + d, 8)], fold.at[k, step, 1, me],
                fold_s.at[k, step, d - 1], fold_r.at[k, step, d - 1], peer(d),
            )
            for d in range(1, 8)
        ]

    fold_steps = ((peer_u, u), (peer_v, zl), (peer_v, zl), (peer_u, u))

    def fold_send(k, step, value):
        peer, me = fold_steps[step]
        fold[k, step, 0] = value.astype(BF16).reshape(8, 16, CH)
        for copy in fold_copies(k, step, peer, me):
            copy.start()
        fold[k, step, 1, me] = fold[k, step, 0, me]

    def fold_take(k, step):
        peer, me = fold_steps[step]
        for copy in fold_copies(k, step, peer, me):
            copy.wait()
        return fold[k, step, 1].reshape(128, CH)

    def fold_first(k, strip):
        fold_send(k, 0, dot(onehot(96, 128, fold_slots), strip, (0, 0)))

    def fold_next(k, step):
        value = fold_take(k, step - 1)

        def facing(p):
            into = p % 16 // 2
            target = into // 2 * 16 + p // 16 * 2 + into % 2
            shift = jnp.where(u == 6, 1, 0) - jnp.where(u == 7, 1, 0)
            source = (part[...] + ia - target + shift + LANES) % LANES
            return source // 2 % 8 * 16 + (source // 16 * 2 + source % 2) * 2 + p % 2

        matrix = onehot(128, 128, facing if step == 2 else fold_swap)
        fold_send(k, step, dot(matrix, value, (0, 0)))

    def fold_last(k):
        return dot(onehot(128, PAD * WIDE, fold_cells), fold_take(k, 3), (0, 0))

    first = halo(state, hw, he, hv, hs, hr)

    @pl.when(top)
    def _():
        fold_first(0, xs[4:7].reshape(96, CH))

    @pl.when(bottom)
    def _():
        hv[0] = jnp.zeros((PAD, COLS, CH), BF16)

    middle, sides = ((8, 16),), ((0, 8), (24, 8))
    own, beyond = tuple(range(PAD, PAD + ROWS)), (0, 1, 2, 11, 12, 13)

    def nothing(ct, j, start, width):
        return jnp.zeros((width, 128), F32)

    def read_acc(ct, j, start, width):
        return acc[ct, j, start : start + width, :]

    def write_acc(ct, lanes, j, start, width, value):
        acc[ct, j, start : start + width, :] = value

    conv_part(wide, taps, False, own, middle, nothing, write_acc)
    for copy in first[2:]:
        copy.wait()
    widen_sides(wide, hw, he)

    @pl.when(top)
    def _():
        fold_next(0, 1)

    conv_part(wide, taps, False, own, sides, nothing, write_acc)

    @pl.when(top)
    def _():
        fold_next(0, 2)
        fold_next(0, 3)

    finish_rows(first)
    second = corners(hv, cw, ce, qs, qr)
    widen_rows(wide, hv, 0)

    @pl.when(jnp.logical_not(top))
    def _():
        widen_rows(wide, hv, 1)

    @pl.when(top)
    def _():
        ghost = fold_last(0)
        for ct in range(3):
            for q in range(PAD):
                wide[ct, ROWS + PAD + q] = ghost[q * WIDE : (q + 1) * WIDE, ct * 128 : ct * 128 + 128]

    def half_pass(k):
        base = k * 128
        block = slice(base, base + 128)
        spans = (middle, sides)[k]
        conv_part(wide, taps, False, beyond, spans, read_acc, write_acc)

        def norm_rows(i, _):
            cells = pl.ds(pl.multiple_of(base + i * 32, 32), 32)
            value = jnp.concatenate(
                [
                    jnp.concatenate(
                        [acc[ct, 2 * i + q, start : start + width, :] for q in range(2) for start, width in spans],
                        axis=0,
                    )
                    for ct in range(3)
                ],
                axis=1,
            )
            value = value - jnp.mean(value, axis=1, keepdims=True)
            r = lax.rsqrt(jnp.mean(value * value, axis=1, keepdims=True) + 1e-06)
            value = value * r
            rstd[cells, :] = r
            unit[cells, :] = value
            normed[cells, :] = (value * gain[...][None] + shift[...][None]).astype(BF16)
            return 0

        lax.fori_loop(0, 4, norm_rows, 0)
        pre[...] = dot(normed[block, :], wup[...])

        def gelu_rows(i, totals):
            here = pl.ds(pl.multiple_of(i * 32, 32), 32)
            cells = pl.ds(pl.multiple_of(base + i * 32, 32), 32)
            done = []
            for q in range(3):
                lanes = slice(q * 256, q * 256 + 256)
                v = pre[here, lanes] + bup[:, lanes]
                square = v * v
                tanh = jnp.tanh(v * (COEFF + COEFF * CUBIC * square))
                half = 0.5 + 0.5 * tanh
                value = v * half
                slope = half + value * (1.0 - tanh) * (COEFF + 3.0 * CUBIC * COEFF * square)
                hidden[cells, lanes] = value.astype(BF16)
                grad = dhid[cells, lanes] * slope
                dpre[cells, lanes] = grad.astype(BF16)
                done.append(totals[q] + sub8(grad))
            return tuple(done)

        bias = lax.fori_loop(0, 4, gelu_rows, tuple(jnp.zeros((8, 256), F32) for _ in range(3)))
        dnorm[...] = dot(dpre[block, :], wup[...], (1, 1))

        def back_rows(i, totals):
            here = pl.ds(pl.multiple_of(i * 32, 32), 32)
            cells = pl.ds(pl.multiple_of(base + i * 32, 32), 32)
            unit_rows = unit[cells, :]
            grad = dnorm[here, :]
            product = grad * unit_rows
            scaled = grad * gain[...][None]
            mean_a = jnp.mean(scaled, axis=1, keepdims=True)
            mean_b = jnp.mean(product * gain[...][None], axis=1, keepdims=True)
            value = rstd[cells, :] * (scaled - mean_a - unit_rows * mean_b)
            value = value.astype(BF16).astype(F32)
            for ct in range(3):
                lanes = slice(ct * 128, ct * 128 + 128)
                at = 0
                for q in range(2):
                    for start, width in spans:
                        dcv[ct, 2 * i + q, start : start + width, :] = value[at : at + width, lanes]
                        at += width
            return totals[0] + sub8(product), totals[1] + sub8(grad)

        zero = jnp.zeros((8, CH), F32)
        return bias, lax.fori_loop(0, 4, back_rows, (zero, zero))

    bias_a, norm_a = half_pass(0)

    finish_corners(wide, second, cw, ce)
    bias_b, norm_b = half_pass(1)

    for ct in range(3):
        for r in range(ROWS):
            dcb[r, :, ct * 128 : ct * 128 + 128] = dcv[ct, r].astype(BF16)

    @pl.when(bottom)
    def _():
        dv[0] = jnp.zeros((PAD, COLS, CH), BF16)

    third = halo(dcb, dw, de, dv, ds, dr)

    @pl.when(top)
    def _():
        fold_first(1, dcb[5:8].reshape(96, CH))

    for half in range(2):
        units = slice(half * 384, half * 384 + 384)
        g[0, half] = dot(dpre[:, units], normed[...], (0, 0)).astype(BF16)
        g[1, half] = dot(dbr[...], hidden[:, units], (0, 0)).astype(BF16)
    cross = remote(g.at[:, 1 - c], gc, cs_s.at[0], cs_r.at[0], other)
    cross.start()

    def tap_tile(ct, _):
        lanes = pl.ds(pl.multiple_of(ct * 128, 128), 128)
        for b in range(KW):
            total = [jnp.zeros((8, 128), F32) for _ in range(KW)]
            for r in range(ROWS + 2 * PAD):
                value = wide[ct, r, 5 + b : 5 + b + COLS, :]
                for a in range(KW):
                    j = r - a
                    if 0 <= j < ROWS:
                        total[a] = total[a] + sub8(value * dcv[ct, j])
            for a in range(KW):
                s[a * KW + b : a * KW + b + 1, lanes] = jnp.sum(total[a], axis=0, keepdims=True)
        return 0

    s[...] = jnp.zeros((64, 512), F32)
    lax.fori_loop(0, 3, tap_tile, 0)

    branch = dot(hidden[...], wdown[...], (1, 1)) + bdown[...][None]
    g_scale = jnp.sum(masked[...] * branch, axis=0, keepdims=True)
    g_bup = jnp.concatenate(
        [jnp.sum(va + vb, axis=0, keepdims=True) for va, vb in zip(bias_a, bias_b)], axis=1
    )
    back = jnp.sum(dot(split3(g_bup), perm[...], (1, 1)), axis=0, keepdims=True)
    s[49:50, 0:CH] = jnp.sum(norm_a[0] + norm_b[0], axis=0, keepdims=True)
    s[50:51, 0:CH] = jnp.sum(norm_a[1] + norm_b[1], axis=0, keepdims=True)
    s[51:52, 0:CH] = jnp.sum(g_bdown, axis=0, keepdims=True)
    s[52:53, 0:CH] = g_scale
    s[53:54, 0:CH] = back[:, 0:CH]
    s[54:55, 0:CH] = back[:, CH:HID]
    half_s = pl.multiple_of((1 - c) * 32, 32)
    cross_s = remote(s.at[pl.ds(half_s, 32)], sc, sa_s.at[0], sa_r.at[0], other)
    cross_s.start()

    cross.wait()
    for k in range(2):
        for q in range(4):
            rows = slice(q * 96, q * 96 + 96)
            h[k, q] = (g[k, c, rows, :].astype(F32) + gc[k, rows, :].astype(F32)).astype(BF16)
    along = []
    for d in range(1, 4):
        up = remote(h.at[0, lax.rem(x + d, 4)], h1.at[0, d - 1], f_s.at[0, d - 1], f_r.at[0, d - 1], peer_x(d))
        down = remote(h.at[1, lax.rem(y + d, 4)], h1.at[1, d - 1], f_s.at[1, d - 1], f_r.at[1, d - 1], peer_y(d))
        up.start()
        down.start()
        along += [up, down]

    cross_s.wait()
    mine_s = pl.multiple_of(c * 32, 32)
    s1[...] = (s[pl.ds(mine_s, 32), :] + sc[...]).reshape(4, 8, 512)
    small = []
    for d in range(1, 4):
        copy = remote(s1.at[lax.rem(x + d, 4)], sx.at[d - 1], sx_s.at[d - 1], sx_r.at[d - 1], peer_x(d))
        copy.start()
        small.append(copy)

    @pl.when(top)
    def _():
        fold_next(1, 1)

    def read_bacc(ct, j, start, width):
        return bacc[ct, j, start : start + width, :]

    def put_back(ct, lanes, j, start, width, value):
        value = cs[j, :, lanes].astype(F32) + value
        gs_out[j, :, lanes] = value.astype(BF16)
        if 4 <= j < 7:
            edge_rows[j - 4, :, lanes] = value

    def write_bacc(ct, lanes, j, start, width, value):
        if 3 <= j < 5:
            put_back(ct, lanes, j, start, width, value)
        else:
            bacc[ct, j, start : start + width, :] = value

    widen_own(dwide, dcb)
    for copy in third[2:]:
        copy.wait()
    widen_sides(dwide, dw, de)
    conv_part(dwide, taps, True, own, ((0, COLS),), nothing, write_bacc)

    for copy in small:
        copy.wait()
    s2[...] = s1[x] + sx[0] + sx[1] + sx[2]
    small = []
    for d in range(1, 4):
        chunk = pl.ds(pl.multiple_of(lax.rem(y + d, 4) * 128, 128), 128)
        copy = remote(s2.at[:, chunk], sy.at[d - 1], sy_s.at[d - 1], sy_r.at[d - 1], peer_y(d))
        copy.start()
        small.append(copy)

    for copy in along:
        copy.wait()
    spread = onehot(CH, 512, lambda p: jnp.where(p % 128 < 96, p // 128 * 96 + p % 128, -1))
    for k in range(2):
        mine = h[k, (x, y)[k]].astype(F32)
        mine = mine + h1[k, 0].astype(F32) + h1[k, 1].astype(F32) + h1[k, 2].astype(F32)
        mine = dot(mine.astype(BF16), spread).astype(BF16)
        for q in range(4):
            h2[k, q] = mine[:, q * 128 : q * 128 + 128]
    along = []
    for d in range(1, 4):
        up = remote(h2.at[0, lax.rem(y + d, 4)], r2.at[0, d - 1], k_s.at[0, d - 1], k_r.at[0, d - 1], peer_y(d))
        down = remote(h2.at[1, lax.rem(x + d, 4)], r2.at[1, d - 1], k_s.at[1, d - 1], k_r.at[1, d - 1], peer_x(d))
        up.start()
        down.start()
        along += [up, down]

    for copy in small:
        copy.wait()
    mine_y = pl.ds(pl.multiple_of(y * 128, 128), 128)
    s3[...] = s2[:, mine_y] + sy[0] + sy[1] + sy[2]
    small = []
    for d in range(1, 16):
        copy = remote(s3, sz.at[z], sz_s.at[d - 1], sz_r.at[d - 1], peer_z(d))
        copy.start()
        small.append(copy)
    sz[z] = s3[...]

    @pl.when(top)
    def _():
        fold_next(1, 2)

    for copy in along:
        copy.wait()
    parts = []
    for k in range(2):
        mine = h2[k, (y, x)[k]].astype(F32)
        mine = mine + r2[k, 0].astype(F32) + r2[k, 1].astype(F32) + r2[k, 2].astype(F32)
        parts.append(mine.astype(BF16))
    pick_up = onehot(128, 256, lambda p: jnp.where(p % 128 < 48, p // 128 * 48 + p % 128, -1))
    pick_down = onehot(
        96, 256, lambda p: jnp.where((p % 128 >= 64) & (p % 128 < 112), p // 128 * 48 + p % 128 - 64, -1)
    )
    both = dot(parts[0], pick_up) + dot(parts[1], pick_down, (0, 0))[0:96]
    rows_to = onehot(96, 128, lambda p: jnp.where(p % 16 < 12, p // 16 * 12 + p % 16, -1))
    tiles = dot(rows_to, both.astype(BF16), (0, 0)).astype(BF16)
    for q in range(16):
        t[q] = tiles[q % 8 * 16 : q % 8 * 16 + 16, q // 8 * 128 : q // 8 * 128 + 128]
    along = []
    for d in range(1, 16):
        copy = remote(t.at[lax.rem(z + d, 16)], tz.at[d - 1], z_s.at[d - 1], z_r.at[d - 1], peer_z(d))
        copy.start()
        along.append(copy)

    finish_rows(third)
    fourth = corners(dv, ew, ee, es, er)
    widen_rows(dwide, dv, 0)

    @pl.when(jnp.logical_not(top))
    def _():
        widen_rows(dwide, dv, 1)

    @pl.when(top)
    def _():
        dwide[:, ROWS + PAD :] = jnp.zeros((3, PAD, WIDE, 128), F32)
        fold_next(1, 3)

    for copy in small:
        copy.wait()
    total = sz[0]
    for q in range(1, 16):
        total = total + sz[q]
    b1[:, mine_y] = total * FACTOR
    gather = []
    for d in range(1, 4):
        copy = remote(b1.at[:, mine_y], b1.at[:, mine_y], gy_s.at[d - 1], gy_r.at[d - 1], peer_y(d))
        copy.start()
        gather.append(copy)

    finish_corners(dwide, fourth, ew, ee)
    conv_part(dwide, taps, True, beyond, ((0, COLS),), read_bacc, put_back)

    for copy in gather:
        copy.wait()
    b2[x] = b1[...]
    gather = []
    for d in range(1, 4):
        copy = remote(b1, b2.at[x], gx_s.at[d - 1], gx_r.at[d - 1], peer_x(d))
        copy.start()
        gather.append(copy)

    for copy in along:
        copy.wait()
    total = t[z].astype(F32)
    for d in range(15):
        total = total + tz[d].astype(F32)
    tile_out[...] = total * FACTOR

    for copy in gather:
        copy.wait()
    b3[c] = b2[...]
    copy = remote(b2, b3.at[c], gc_s.at[0], gc_r.at[0], other)
    copy.start()

    @pl.when(top)
    def _():
        ghost = fold_last(1)
        for ct in range(3):
            for q in range(PAD):
                edge[ct, q] = ghost[q * WIDE : (q + 1) * WIDE, ct * 128 : ct * 128 + 128]

        def read_edge(j, lanes):
            return edge_rows[j, :, lanes]

        def put_edge(j, lanes, value):
            gs_out[4 + j, :, lanes] = value.astype(BF16)

        fold_into(edge, taps, read_edge, put_edge)

    copy.wait()
    small_out[...] = b3[...].reshape(64, 512)


def finish(gs_in, tile_in, small_in, gs_out, up_out, down_out, gk_out, gc_out, gb_out):
    gs_out[...] = gs_in[...]
    up_out[...] = tile_in[0:12, 0:48]
    down_out[...] = tile_in[0:12, 64:112]
    gk_out[...] = small_in[0:49, 0:CH]
    gc_out[...] = small_in[49:53, 0:CH]
    gb_out[0:CH] = small_in[53, 0:CH]
    gb_out[CH:HID] = small_in[54, 0:CH]


def fused(*args):
    sds = jax.ShapeDtypeStruct
    vm = pltpu.VMEM
    dma = pltpu.SemaphoreType.DMA
    hbm_spec = pl.BlockSpec(memory_space=pltpu.HBM)
    vm_spec = pl.BlockSpec(memory_space=pltpu.VMEM)
    edge16 = (ROWS, 16, CH)
    corner = (2, PAD, 16, CH)
    scratch = [
        vm((ROWS, COLS, CH), BF16), vm((ROWS, COLS, CH), BF16), vm((ROWS, COLS), jnp.int32), vm((1, 1), jnp.int32),
        vm((49, CH), F32), vm((CH,), F32), vm((CH,), F32), vm((CH, HID), BF16), vm((HID,), F32),
        vm((CH, HID), BF16), vm((CH,), F32), vm((CH,), F32),
        vm(edge16, BF16), vm(edge16, BF16), vm((2, PAD, COLS, CH), BF16), vm(corner, BF16), vm(corner, BF16),
        vm(edge16, BF16), vm(edge16, BF16), vm((2, PAD, COLS, CH), BF16), vm(corner, BF16), vm(corner, BF16),
        vm((3, 14, WIDE, 128), F32), vm((3, 14, WIDE, 128), F32), vm((3, PAD, WIDE, 128), F32),
        vm((3, ROWS, COLS, 128), F32), vm((3, ROWS, COLS, 128), F32), vm((PAD, COLS, CH), F32),
        vm((CH, HID), BF16), vm((CH, HID), BF16), vm((1, HID), F32),
        vm((CELLS, CH), F32), vm((CELLS, 1), F32), vm((CELLS, CH), BF16),
        vm((CELLS, CH), F32), vm((CELLS, CH), BF16), vm((CELLS, HID), F32), vm((CELLS // 2, HID), F32),
        vm((CELLS, HID), BF16), vm((CELLS, HID), BF16), vm((CELLS // 2, CH), F32),
        vm((3, ROWS, COLS, 128), F32), vm((ROWS, COLS, CH), BF16),
        vm((2, 2, 384, 384), BF16), vm((2, 384, 384), BF16), vm((2, 4, 96, 384), BF16),
        vm((2, 3, 96, 384), BF16), vm((2, 4, 96, 128), BF16), vm((2, 3, 96, 128), BF16),
        vm((16, 16, 128), BF16), vm((15, 16, 128), BF16), vm((HID, HID), BF16),
        vm((64, 512), F32), vm((32, 512), F32), vm((4, 8, 512), F32), vm((3, 8, 512), F32), vm((8, 512), F32),
        vm((3, 8, 128), F32), vm((8, 128), F32), vm((16, 8, 128), F32), vm((8, 512), F32), vm((4, 8, 512), F32),
        vm((2, 4, 8, 512), F32), vm((2, 4, 2, 8, 16, CH), BF16),
        dma((12,)), dma((4,)), dma((4,)), dma((4,)), dma((4,)), dma((4,)), dma((4,)), dma((4,)), dma((4,)),
        dma((1,)), dma((1,)), dma((2, 3)), dma((2, 3)), dma((2, 3)), dma((2, 3)), dma((15,)), dma((15,)),
        dma((1,)), dma((1,)), dma((3,)), dma((3,)), dma((3,)), dma((3,)), dma((15,)), dma((15,)),
        dma((3,)), dma((3,)), dma((3,)), dma((3,)), dma((1,)), dma((1,)), dma((2, 4, 7)), dma((2, 4, 7)),
    ]
    return pl.pallas_call(
        body,
        out_shape=[sds((ROWS, COLS, CH), BF16), sds((16, 128), F32), sds((64, 512), F32)],
        in_specs=[hbm_spec] * 12,
        out_specs=[vm_spec] * 3,
        scratch_shapes=scratch,
        compiler_params=pltpu.CompilerParams(
            collective_id=0, has_side_effects=True, vmem_limit_bytes=63 * 2**20
        ),
        name="block",
    )(*args)


def local(
    state, cotangent, ocean, fold_partner, kernel, ln_gain, ln_shift, w_up, b_up, w_down, b_down, layer_scale
):
    results = fused(
        state, cotangent, ocean, fold_partner[None], kernel, ln_gain, ln_shift, w_up, b_up,
        w_down, b_down, layer_scale,
    )
    sds = jax.ShapeDtypeStruct
    grad_state, up, down, g_kernel, g_chan, g_bup = (
        pl.pallas_call(
            finish,
            out_shape=[
                sds((ROWS, COLS, CH), BF16), sds((12, 48), F32), sds((12, 48), F32),
                sds((49, CH), F32), sds((4, CH), F32), sds((HID,), F32),
            ],
            name="outputs",
        )(*results)
    )
    return grad_state, up.T, down.T, g_kernel, g_chan, g_bup


def solution(mesh):
    placed = (P("ja", "ia", None), P("ja", "ia", None), P("ja", "ia"), P("ia")) + (P(),) * 8
    return jax.shard_map(
        local,
        mesh=mesh,
        in_specs=placed,
        out_specs=(P("ja", "ia", None), P("ja", "ia"), P("ja", "ia"), P(), P(), P()),
        check_vma=False,
    )
```

time: 170 us -> 99.3 us (0.58)
  the two profiles are of different devices: /device:TPU:409 before, /device:TPU:1 now
where the time goes in v2:
time: 99.3 us; the launch traced here: 99.1 us
  Pallas kernels  97.8 us (98%)
  between operations  1.29 us (1%)
    pallas_call x1, Pallas kernels, fused(): pl.pallas_call(body, out_shape=[sds((ROWS, COLS, CH), BF16), sds((16, 128...  96.1 us

profile of v2, /device:TPU:1, one launch (start us, length us, event | category | flops | bytes accessed | tf_op | source)
XLA Modules:
  0.0 99.1 jit_solution(14941752153662778683)
XLA Ops:
  1.3 96.1 %block.1 = (bf16[8,32,384]{2,1,0:T(8,128)(2,1)}, f32[16,128]{1,0:T(8,128)}, f32[64,512]{1,0:T(8,128)}) custom-call(bf16[8,32,384]{2,1,0:T(8,128)(2,1)} %state.1, bf16[8,32,384]{2,1,0:T(8,128)(2,1)} %cot.1, s32[8,32]{1,0:T(8,128)} %ocean.1, s32[1,1]{1,0:T(1,128)} %bitcast.3.partner, f32[49,384]{1,0:T(8,128)} %taps_in.1, f32[384]{0:T(512)} %gain_in.1, ...), custom_call_target="tpu_custom_call" | custom-call | tf_op jit(solution)/shard_map/block/pallas_call | solution.py:769
  97.4 1.7 %outputs.1 = (bf16[8,32,384]{2,1,0:T(8,128)(2,1)}, f32[12,48]{1,0:T(8,128)}, f32[12,48]{1,0:T(8,128)}, f32[49,384]{1,0:T(8,128)}, f32[4,384]{1,0:T(4,128)}, /*index=5*/f32[768]{0:T(1024)}) custom-call(bf16[8,32,384]{2,1,0:T(8,128)(2,1)} %get-tuple-element.15.gs_in, f32[16,128]{1,0:T(8,128)} %get-tuple-element.16.tile_in, f32[64,512]{1,0:T(8,128)} %get-tuple-element.17.small_in), custom_call_target="tpu_custom_call" | custom-call | tf_op jit(solution)/shard_map/outputs/pallas_call | solution.py:791

commit v3 on v2

--- a/solution.py
+++ b/solution.py
@@ -56,25 +56,24 @@
     ).astype(BF16)
 
 
-def conv_part(wide, taps, flip, rows, spans, read, write):
+def conv_part(wide, taps, flip, rows, outs, read, write):
     def tile(ct, _):
         lanes = pl.ds(pl.multiple_of(ct * 128, 128), 128)
-        for start, width in spans:
-            hit = [j for j in range(ROWS) if any(0 <= r - j < KW for r in rows)]
-            total = {j: read(ct, j, start, width) for j in hit}
-            for b in range(KW):
-                weight = []
+        hit = [j for j in outs if any(0 <= r - j < KW for r in rows)]
+        total = {j: read(ct, j) for j in hit}
+        for b in range(KW):
+            weight = []
+            for a in range(KW):
+                tap = a * KW + b
+                tap = KW * KW - 1 - tap if flip else tap
+                weight.append(taps[tap : tap + 1, lanes])
+            for r in rows:
+                value = wide[ct, r, 5 + b : 5 + b + COLS, :]
                 for a in range(KW):
-                    tap = a * KW + b
-                    tap = KW * KW - 1 - tap if flip else tap
-                    weight.append(taps[tap : tap + 1, lanes])
-                for r in rows:
-                    value = wide[ct, r, 5 + b + start : 5 + b + start + width, :]
-                    for a in range(KW):
-                        if r - a in total:
-                            total[r - a] = total[r - a] + value * weight[a]
-            for j in hit:
-                write(ct, lanes, j, start, width, total[j])
+                    if r - a in total:
+                        total[r - a] = total[r - a] + value * weight[a]
+        for j in hit:
+            write(ct, lanes, j, total[j])
         return 0
 
     lax.fori_loop(0, 3, tile, 0)
@@ -218,12 +217,10 @@
 
     def mask_row(j, total):
         sea = jnp.sum(eye * oc[pl.ds(j, 1), :].astype(F32), axis=1, keepdims=True)
+        cells = pl.ds(pl.multiple_of(j * COLS, COLS), COLS)
         value = cs[j].astype(F32) * sea
-        halves = (value[8:24], jnp.concatenate([value[0:8], value[24:32]], axis=0))
-        for k in range(2):
-            cells = pl.ds(pl.multiple_of(k * 128 + j * 16, 16), 16)
-            masked[cells, :] = halves[k]
-            dbr[cells, :] = (halves[k] * scale[...][None]).astype(BF16)
+        masked[cells, :] = value
+        dbr[cells, :] = (value * scale[...][None]).astype(BF16)
         return total + sub8(value * scale[...][None])
 
     g_bdown = lax.fori_loop(0, ROWS, mask_row, jnp.zeros((8, CH), F32))
@@ -260,56 +257,67 @@
     pl.semaphore_wait(barrier, 26 + jnp.where(top, 14, 0))
 
     def halo(src, w, e, v, send, recv):
-        to_north = remote(src.at[5:8], v.at[0], send.at[0], recv.at[0], north)
-        to_south = remote(src.at[0:3], v.at[1], send.at[1], recv.at[1], south)
-        to_east = remote(src.at[:, 16:32], w, send.at[2], recv.at[2], east)
-        to_west = remote(src.at[:, 0:16], e, send.at[3], recv.at[3], west)
-
+        return (
+            remote(src.at[5:8], v.at[0], send.at[0], recv.at[0], north),
+            remote(src.at[0:3], v.at[1], send.at[1], recv.at[1], south),
+            remote(src.at[:, 16:32], w, send.at[2], recv.at[2], east),
+            remote(src.at[:, 0:16], e, send.at[3], recv.at[3], west),
+        )
+
+    def start_south(copies):
+        @pl.when(jnp.logical_not(bottom))
+        def _():
+            copies[1].start()
+
+    def start_rest(copies):
         @pl.when(jnp.logical_not(top))
         def _():
-            to_north.start()
-
+            copies[0].start()
+
+        copies[2].start()
+        copies[3].start()
+
+    def finish_south(copies):
         @pl.when(jnp.logical_not(bottom))
         def _():
-            to_south.start()
-
-        to_east.start()
-        to_west.start()
-        return to_north, to_south, to_east, to_west
-
-    def finish_rows(copies):
-        to_north, to_south, _, _ = copies
-
+            copies[1].wait_send()
+            copies[0].wait_recv()
+
+    def finish_north(copies):
         @pl.when(jnp.logical_not(top))
         def _():
-            to_north.wait_send()
-            to_south.wait_recv()
-
-        @pl.when(jnp.logical_not(bottom))
-        def _():
-            to_south.wait_send()
-            to_north.wait_recv()
+            copies[0].wait_send()
+            copies[1].wait_recv()
 
     def corners(v, w, e, send, recv):
         copies = []
         for k in range(2):
             copies.append(remote(v.at[k, :, 16:32], w.at[k], send.at[2 * k], recv.at[2 * k], east))
             copies.append(remote(v.at[k, :, 0:16], e.at[k], send.at[2 * k + 1], recv.at[2 * k + 1], west))
-        copies[0].start()
-        copies[1].start()
+        return copies
+
+    def rows_arrived(dst, copies, v, w, e, send, recv):
+        passed = corners(v, w, e, send, recv)
+        finish_south(copies)
+        passed[0].start()
+        passed[1].start()
+        widen_rows(dst, v, 0)
+        finish_north(copies)
 
         @pl.when(jnp.logical_not(top))
         def _():
-            copies[2].start()
-            copies[3].start()
-
-        return copies
-
-    def finish_corners(dst, copies, w, e):
+            passed[2].start()
+            passed[3].start()
+            widen_rows(dst, v, 1)
+
+        return passed
+
+    def finish_corners_south(dst, copies, w, e):
         copies[0].wait()
         copies[1].wait()
         widen_corners(dst, w, e, 0)
 
+    def finish_corners_north(dst, copies, w, e):
         @pl.when(jnp.logical_not(top))
         def _():
             copies[2].wait()
@@ -360,6 +368,8 @@
         return dot(onehot(128, PAD * WIDE, fold_cells), fold_take(k, 3), (0, 0))
 
     first = halo(state, hw, he, hv, hs, hr)
+    start_south(first)
+    start_rest(first)
 
     @pl.when(top)
     def _():
@@ -369,19 +379,18 @@
     def _():
         hv[0] = jnp.zeros((PAD, COLS, CH), BF16)
 
-    middle, sides = ((8, 16),), ((0, 8), (24, 8))
-    own, beyond = tuple(range(PAD, PAD + ROWS)), (0, 1, 2, 11, 12, 13)
-
-    def nothing(ct, j, start, width):
-        return jnp.zeros((width, 128), F32)
-
-    def read_acc(ct, j, start, width):
-        return acc[ct, j, start : start + width, :]
-
-    def write_acc(ct, lanes, j, start, width, value):
-        acc[ct, j, start : start + width, :] = value
-
-    conv_part(wide, taps, False, own, middle, nothing, write_acc)
+    own, south_rows, north_rows = tuple(range(PAD, PAD + ROWS)), (0, 1, 2), (11, 12, 13)
+    every = tuple(range(ROWS))
+
+    def nothing(ct, j):
+        return jnp.zeros((COLS, 128), F32)
+
+    def read_acc(ct, j):
+        return acc[ct, j]
+
+    def write_acc(ct, lanes, j, value):
+        acc[ct, j] = value
+
     for copy in first[2:]:
         copy.wait()
     widen_sides(wide, hw, he)
@@ -390,46 +399,27 @@
     def _():
         fold_next(0, 1)
 
-    conv_part(wide, taps, False, own, sides, nothing, write_acc)
+    conv_part(wide, taps, False, own, every, nothing, write_acc)
 
     @pl.when(top)
     def _():
         fold_next(0, 2)
+
+    second = rows_arrived(wide, first, hv, cw, ce, qs, qr)
+
+    @pl.when(top)
+    def _():
         fold_next(0, 3)
-
-    finish_rows(first)
-    second = corners(hv, cw, ce, qs, qr)
-    widen_rows(wide, hv, 0)
-
-    @pl.when(jnp.logical_not(top))
-    def _():
-        widen_rows(wide, hv, 1)
-
-    @pl.when(top)
-    def _():
-        ghost = fold_last(0)
-        for ct in range(3):
-            for q in range(PAD):
-                wide[ct, ROWS + PAD + q] = ghost[q * WIDE : (q + 1) * WIDE, ct * 128 : ct * 128 + 128]
 
     def half_pass(k):
         base = k * 128
         block = slice(base, base + 128)
-        spans = (middle, sides)[k]
-        conv_part(wide, taps, False, beyond, spans, read_acc, write_acc)
+        beyond = (south_rows, north_rows)[k]
+        conv_part(wide, taps, False, beyond, every[4 * k : 4 * k + 4], read_acc, write_acc)
 
         def norm_rows(i, _):
             cells = pl.ds(pl.multiple_of(base + i * 32, 32), 32)
-            value = jnp.concatenate(
-                [
-                    jnp.concatenate(
-                        [acc[ct, 2 * i + q, start : start + width, :] for q in range(2) for start, width in spans],
-                        axis=0,
-                    )
-                    for ct in range(3)
-                ],
-                axis=1,
-            )
+            value = jnp.concatenate([acc[ct, 4 * k + i] for ct in range(3)], axis=1)
             value = value - jnp.mean(value, axis=1, keepdims=True)
             r = lax.rsqrt(jnp.mean(value * value, axis=1, keepdims=True) + 1e-06)
             value = value * r
@@ -472,44 +462,41 @@
             mean_a = jnp.mean(scaled, axis=1, keepdims=True)
             mean_b = jnp.mean(product * gain[...][None], axis=1, keepdims=True)
             value = rstd[cells, :] * (scaled - mean_a - unit_rows * mean_b)
-            value = value.astype(BF16).astype(F32)
+            value = value.astype(BF16)
+            dcb[4 * k + i] = value
+            value = value.astype(F32)
             for ct in range(3):
-                lanes = slice(ct * 128, ct * 128 + 128)
-                at = 0
-                for q in range(2):
-                    for start, width in spans:
-                        dcv[ct, 2 * i + q, start : start + width, :] = value[at : at + width, lanes]
-                        at += width
+                dcv[ct, 4 * k + i] = value[:, ct * 128 : ct * 128 + 128]
             return totals[0] + sub8(product), totals[1] + sub8(grad)
 
         zero = jnp.zeros((8, CH), F32)
         return bias, lax.fori_loop(0, 4, back_rows, (zero, zero))
 
+    @pl.when(bottom)
+    def _():
+        dv[0] = jnp.zeros((PAD, COLS, CH), BF16)
+
+    finish_corners_south(wide, second, cw, ce)
     bias_a, norm_a = half_pass(0)
-
-    finish_corners(wide, second, cw, ce)
+    third = halo(dcb, dw, de, dv, ds, dr)
+    start_south(third)
+
+    finish_corners_north(wide, second, cw, ce)
+
+    @pl.when(top)
+    def _():
+        ghost = fold_last(0)
+        for ct in range(3):
+            for q in range(PAD):
+                wide[ct, ROWS + PAD + q] = ghost[q * WIDE : (q + 1) * WIDE, ct * 128 : ct * 128 + 128]
+
     bias_b, norm_b = half_pass(1)
 
-    for ct in range(3):
-        for r in range(ROWS):
-            dcb[r, :, ct * 128 : ct * 128 + 128] = dcv[ct, r].astype(BF16)
-
-    @pl.when(bottom)
-    def _():
-        dv[0] = jnp.zeros((PAD, COLS, CH), BF16)
-
-    third = halo(dcb, dw, de, dv, ds, dr)
+    start_rest(third)
 
     @pl.when(top)
     def _():
         fold_first(1, dcb[5:8].reshape(96, CH))
-
-    for half in range(2):
-        units = slice(half * 384, half * 384 + 384)
-        g[0, half] = dot(dpre[:, units], normed[...], (0, 0)).astype(BF16)
-        g[1, half] = dot(dbr[...], hidden[:, units], (0, 0)).astype(BF16)
-    cross = remote(g.at[:, 1 - c], gc, cs_s.at[0], cs_r.at[0], other)
-    cross.start()
 
     def tap_tile(ct, _):
         lanes = pl.ds(pl.multiple_of(ct * 128, 128), 128)
@@ -544,6 +531,22 @@
     cross_s = remote(s.at[pl.ds(half_s, 32)], sc, sa_s.at[0], sa_r.at[0], other)
     cross_s.start()
 
+    for half in range(2):
+        units = slice(half * 384, half * 384 + 384)
+        g[0, half] = dot(dpre[:, units], normed[...], (0, 0)).astype(BF16)
+        g[1, half] = dot(dbr[...], hidden[:, units], (0, 0)).astype(BF16)
+    cross = remote(g.at[:, 1 - c], gc, cs_s.at[0], cs_r.at[0], other)
+    cross.start()
+
+    cross_s.wait()
+    mine_s = pl.multiple_of(c * 32, 32)
+    s1[...] = (s[pl.ds(mine_s, 32), :] + sc[...]).reshape(4, 8, 512)
+    small = []
+    for d in range(1, 4):
+        copy = remote(s1.at[lax.rem(x + d, 4)], sx.at[d - 1], sx_s.at[d - 1], sx_r.at[d - 1], peer_x(d))
+        copy.start()
+        small.append(copy)
+
     cross.wait()
     for k in range(2):
         for q in range(4):
@@ -557,39 +560,22 @@
         down.start()
         along += [up, down]
 
-    cross_s.wait()
-    mine_s = pl.multiple_of(c * 32, 32)
-    s1[...] = (s[pl.ds(mine_s, 32), :] + sc[...]).reshape(4, 8, 512)
-    small = []
-    for d in range(1, 4):
-        copy = remote(s1.at[lax.rem(x + d, 4)], sx.at[d - 1], sx_s.at[d - 1], sx_r.at[d - 1], peer_x(d))
-        copy.start()
-        small.append(copy)
-
-    @pl.when(top)
-    def _():
-        fold_next(1, 1)
-
-    def read_bacc(ct, j, start, width):
-        return bacc[ct, j, start : start + width, :]
-
-    def put_back(ct, lanes, j, start, width, value):
+    def put_back(ct, lanes, j, value):
         value = cs[j, :, lanes].astype(F32) + value
         gs_out[j, :, lanes] = value.astype(BF16)
         if 4 <= j < 7:
             edge_rows[j - 4, :, lanes] = value
 
-    def write_bacc(ct, lanes, j, start, width, value):
+    def write_bacc(ct, lanes, j, value):
         if 3 <= j < 5:
-            put_back(ct, lanes, j, start, width, value)
+            put_back(ct, lanes, j, value)
         else:
-            bacc[ct, j, start : start + width, :] = value
+            bacc[ct, j] = value
+
+    def read_bacc(ct, j):
+        return bacc[ct, j]
 
     widen_own(dwide, dcb)
-    for copy in third[2:]:
-        copy.wait()
-    widen_sides(dwide, dw, de)
-    conv_part(dwide, taps, True, own, ((0, COLS),), nothing, write_bacc)
 
     for copy in small:
         copy.wait()
@@ -600,6 +586,22 @@
         copy = remote(s2.at[:, chunk], sy.at[d - 1], sy_s.at[d - 1], sy_r.at[d - 1], peer_y(d))
         copy.start()
         small.append(copy)
+
+    for copy in third[2:]:
+        copy.wait()
+    widen_sides(dwide, dw, de)
+    conv_part(dwide, taps, True, own, every, nothing, write_bacc)
+
+    for copy in small:
+        copy.wait()
+    mine_y = pl.ds(pl.multiple_of(y * 128, 128), 128)
+    s3[...] = s2[:, mine_y] + sy[0] + sy[1] + sy[2]
+    small = []
+    for d in range(1, 16):
+        copy = remote(s3, sz.at[z], sz_s.at[d - 1], sz_r.at[d - 1], peer_z(d))
+        copy.start()
+        small.append(copy)
+    sz[z] = s3[...]
 
     for copy in along:
         copy.wait()
@@ -618,20 +620,9 @@
         down.start()
         along += [up, down]
 
-    for copy in small:
-        copy.wait()
-    mine_y = pl.ds(pl.multiple_of(y * 128, 128), 128)
-    s3[...] = s2[:, mine_y] + sy[0] + sy[1] + sy[2]
-    small = []
-    for d in range(1, 16):
-        copy = remote(s3, sz.at[z], sz_s.at[d - 1], sz_r.at[d - 1], peer_z(d))
-        copy.start()
-        small.append(copy)
-    sz[z] = s3[...]
-
-    @pl.when(top)
-    def _():
-        fold_next(1, 2)
+    @pl.when(top)
+    def _():
+        fold_next(1, 1)
 
     for copy in along:
         copy.wait()
@@ -655,18 +646,15 @@
         copy.start()
         along.append(copy)
 
-    finish_rows(third)
-    fourth = corners(dv, ew, ee, es, er)
-    widen_rows(dwide, dv, 0)
-
-    @pl.when(jnp.logical_not(top))
-    def _():
-        widen_rows(dwide, dv, 1)
+    fourth = rows_arrived(dwide, third, dv, ew, ee, es, er)
 
     @pl.when(top)
     def _():
         dwide[:, ROWS + PAD :] = jnp.zeros((3, PAD, WIDE, 128), F32)
-        fold_next(1, 3)
+
+    @pl.when(top)
+    def _():
+        fold_next(1, 2)
 
     for copy in small:
         copy.wait()
@@ -680,9 +668,6 @@
         copy.start()
         gather.append(copy)
 
-    finish_corners(dwide, fourth, ew, ee)
-    conv_part(dwide, taps, True, beyond, ((0, COLS),), read_bacc, put_back)
-
     for copy in gather:
         copy.wait()
     b2[x] = b1[...]
@@ -692,6 +677,20 @@
         copy.start()
         gather.append(copy)
 
+    @pl.when(top)
+    def _():
+        fold_next(1, 3)
+
+    finish_corners_south(dwide, fourth, ew, ee)
+    finish_corners_north(dwide, fourth, ew, ee)
+    conv_part(dwide, taps, True, south_rows + north_rows, every, read_bacc, put_back)
+
+    for copy in gather:
+        copy.wait()
+    b3[c] = b2[...]
+    last = remote(b2, b3.at[c], gc_s.at[0], gc_r.at[0], other)
+    last.start()
+
     for copy in along:
         copy.wait()
     total = t[z].astype(F32)
@@ -699,12 +698,6 @@
         total = total + tz[d].astype(F32)
     tile_out[...] = total * FACTOR
 
-    for copy in gather:
-        copy.wait()
-    b3[c] = b2[...]
-    copy = remote(b2, b3.at[c], gc_s.at[0], gc_r.at[0], other)
-    copy.start()
-
     @pl.when(top)
     def _():
         ghost = fold_last(1)
@@ -720,7 +713,7 @@
 
         fold_into(edge, taps, read_edge, put_edge)
 
-    copy.wait()
+    last.wait()
     small_out[...] = b3[...].reshape(64, 512)
 
 

time: 99.3 us -> 93.6 us (0.943)
  Pallas kernels: 97.8 us -> 92.1 us
    pallas_call x1, Pallas kernels: 96.1 us -> 90.4 us  [fused(): pl.pallas_call(body, out_shape=[sds((ROWS, COLS, CH), BF16), sds((16, 128...]
where the time goes in v3:
time: 93.6 us; the launch traced here: 93.4 us
  Pallas kernels  92.1 us (98%)
  between operations  1.29 us (1%)
    pallas_call x1, Pallas kernels, fused(): pl.pallas_call(body, out_shape=[sds((ROWS, COLS, CH), BF16), sds((16, 128...  90.4 us

profile of v3, /device:TPU:1, one launch (start us, length us, event | category | flops | bytes accessed | tf_op | source)
XLA Modules:
  0.0 93.4 jit_solution(17842133835489364685)
XLA Ops:
  1.3 90.4 %block.1 = (bf16[8,32,384]{2,1,0:T(8,128)(2,1)}, f32[16,128]{1,0:T(8,128)}, f32[64,512]{1,0:T(8,128)}) custom-call(bf16[8,32,384]{2,1,0:T(8,128)(2,1)} %state.1, bf16[8,32,384]{2,1,0:T(8,128)(2,1)} %cot.1, s32[8,32]{1,0:T(8,128)} %ocean.1, s32[1,1]{1,0:T(1,128)} %bitcast.3.partner, f32[49,384]{1,0:T(8,128)} %taps_in.1, f32[384]{0:T(512)} %gain_in.1, ...), custom_call_target="tpu_custom_call" | custom-call | tf_op jit(solution)/shard_map/block/pallas_call | solution.py:762
  91.7 1.7 %outputs.1 = (bf16[8,32,384]{2,1,0:T(8,128)(2,1)}, f32[12,48]{1,0:T(8,128)}, f32[12,48]{1,0:T(8,128)}, f32[49,384]{1,0:T(8,128)}, f32[4,384]{1,0:T(4,128)}, /*index=5*/f32[768]{0:T(1024)}) custom-call(bf16[8,32,384]{2,1,0:T(8,128)(2,1)} %get-tuple-element.15.gs_in, f32[16,128]{1,0:T(8,128)} %get-tuple-element.16.tile_in, f32[64,512]{1,0:T(8,128)} %get-tuple-element.17.small_in), custom_call_target="tpu_custom_call" | custom-call | tf_op jit(solution)/shard_map/outputs/pallas_call | solution.py:784

commit v4 on v3

--- a/solution.py
+++ b/solution.py
@@ -254,76 +254,6 @@
 
     widen_own(wide, xs)
 
-    pl.semaphore_wait(barrier, 26 + jnp.where(top, 14, 0))
-
-    def halo(src, w, e, v, send, recv):
-        return (
-            remote(src.at[5:8], v.at[0], send.at[0], recv.at[0], north),
-            remote(src.at[0:3], v.at[1], send.at[1], recv.at[1], south),
-            remote(src.at[:, 16:32], w, send.at[2], recv.at[2], east),
-            remote(src.at[:, 0:16], e, send.at[3], recv.at[3], west),
-        )
-
-    def start_south(copies):
-        @pl.when(jnp.logical_not(bottom))
-        def _():
-            copies[1].start()
-
-    def start_rest(copies):
-        @pl.when(jnp.logical_not(top))
-        def _():
-            copies[0].start()
-
-        copies[2].start()
-        copies[3].start()
-
-    def finish_south(copies):
-        @pl.when(jnp.logical_not(bottom))
-        def _():
-            copies[1].wait_send()
-            copies[0].wait_recv()
-
-    def finish_north(copies):
-        @pl.when(jnp.logical_not(top))
-        def _():
-            copies[0].wait_send()
-            copies[1].wait_recv()
-
-    def corners(v, w, e, send, recv):
-        copies = []
-        for k in range(2):
-            copies.append(remote(v.at[k, :, 16:32], w.at[k], send.at[2 * k], recv.at[2 * k], east))
-            copies.append(remote(v.at[k, :, 0:16], e.at[k], send.at[2 * k + 1], recv.at[2 * k + 1], west))
-        return copies
-
-    def rows_arrived(dst, copies, v, w, e, send, recv):
-        passed = corners(v, w, e, send, recv)
-        finish_south(copies)
-        passed[0].start()
-        passed[1].start()
-        widen_rows(dst, v, 0)
-        finish_north(copies)
-
-        @pl.when(jnp.logical_not(top))
-        def _():
-            passed[2].start()
-            passed[3].start()
-            widen_rows(dst, v, 1)
-
-        return passed
-
-    def finish_corners_south(dst, copies, w, e):
-        copies[0].wait()
-        copies[1].wait()
-        widen_corners(dst, w, e, 0)
-
-    def finish_corners_north(dst, copies, w, e):
-        @pl.when(jnp.logical_not(top))
-        def _():
-            copies[2].wait()
-            copies[3].wait()
-            widen_corners(dst, w, e, 1)
-
     def fold_copies(k, step, peer, me):
         return [
             remote(
@@ -335,12 +265,18 @@
 
     fold_steps = ((peer_u, u), (peer_v, zl), (peer_v, zl), (peer_u, u))
 
-    def fold_send(k, step, value):
+    def fold_put(k, step, value):
+        fold[k, step, 0] = value.astype(BF16).reshape(8, 16, CH)
+
+    def fold_start(k, step):
         peer, me = fold_steps[step]
-        fold[k, step, 0] = value.astype(BF16).reshape(8, 16, CH)
         for copy in fold_copies(k, step, peer, me):
             copy.start()
         fold[k, step, 1, me] = fold[k, step, 0, me]
+
+    def fold_send(k, step, value):
+        fold_put(k, step, value)
+        fold_start(k, step)
 
     def fold_take(k, step):
         peer, me = fold_steps[step]
@@ -349,7 +285,7 @@
         return fold[k, step, 1].reshape(128, CH)
 
     def fold_first(k, strip):
-        fold_send(k, 0, dot(onehot(96, 128, fold_slots), strip, (0, 0)))
+        fold_put(k, 0, dot(onehot(96, 128, fold_slots), strip, (0, 0)))
 
     def fold_next(k, step):
         value = fold_take(k, step - 1)
@@ -367,13 +303,92 @@
     def fold_last(k):
         return dot(onehot(128, PAD * WIDE, fold_cells), fold_take(k, 3), (0, 0))
 
+    @pl.when(top)
+    def _():
+        fold_first(0, xs[4:7].reshape(96, CH))
+
+    pl.semaphore_wait(barrier, 26 + jnp.where(top, 14, 0))
+
+    def halo(src, w, e, v, send, recv):
+        return (
+            remote(src.at[5:8], v.at[0], send.at[0], recv.at[0], north),
+            remote(src.at[0:3], v.at[1], send.at[1], recv.at[1], south),
+            remote(src.at[:, 16:32], w, send.at[2], recv.at[2], east),
+            remote(src.at[:, 0:16], e, send.at[3], recv.at[3], west),
+        )
+
+    def start_south(copies):
+        @pl.when(jnp.logical_not(bottom))
+        def _():
+            copies[1].start()
+
+    def start_rest(copies):
+        @pl.when(jnp.logical_not(top))
+        def _():
+            copies[0].start()
+
+        copies[2].start()
+        copies[3].start()
+
+    def finish_south(copies):
+        @pl.when(jnp.logical_not(bottom))
+        def _():
+            copies[1].wait_send()
+            copies[0].wait_recv()
+
+    def finish_north(copies):
+        @pl.when(jnp.logical_not(top))
+        def _():
+            copies[0].wait_send()
+            copies[1].wait_recv()
+
+    def corners(v, w, e, send, recv):
+        copies = []
+        for k in range(2):
+            copies.append(remote(v.at[k, :, 16:32], w.at[k], send.at[2 * k], recv.at[2 * k], east))
+            copies.append(remote(v.at[k, :, 0:16], e.at[k], send.at[2 * k + 1], recv.at[2 * k + 1], west))
+        return copies
+
+    def rows_arrived(dst, copies, v, w, e, send, recv):
+        passed = corners(v, w, e, send, recv)
+        finish_south(copies)
+        passed[0].start()
+        passed[1].start()
+        widen_rows(dst, v, 0)
+        finish_north(copies)
+
+        @pl.when(jnp.logical_not(top))
+        def _():
+            passed[2].start()
+            passed[3].start()
+            widen_rows(dst, v, 1)
+
+        return passed
+
+    def finish_corners_south(dst, copies, w, e):
+        copies[0].wait()
+        copies[1].wait()
+        widen_corners(dst, w, e, 0)
+
+    def finish_corners_north(dst, copies, w, e):
+        @pl.when(jnp.logical_not(top))
+        def _():
+            copies[2].wait()
+            copies[3].wait()
+            widen_corners(dst, w, e, 1)
+
     first = halo(state, hw, he, hv, hs, hr)
+
+    @pl.when(top)
+    def _():
+        fold_start(0, 0)
+
     start_south(first)
     start_rest(first)
 
     @pl.when(top)
     def _():
-        fold_first(0, xs[4:7].reshape(96, CH))
+        fold_next(0, 1)
 
     @pl.when(bottom)
     def _():
@@ -394,11 +409,6 @@
     for copy in first[2:]:
         copy.wait()
     widen_sides(wide, hw, he)
-
-    @pl.when(top)
-    def _():
-        fold_next(0, 1)
-
     conv_part(wide, taps, False, own, every, nothing, write_acc)
 
     @pl.when(top)
@@ -428,7 +438,7 @@
             normed[cells, :] = (value * gain[...][None] + shift[...][None]).astype(BF16)
             return 0
 
-        lax.fori_loop(0, 4, norm_rows, 0)
+        lax.fori_loop(0, 4, norm_rows, 0, unroll=True)
         pre[...] = dot(normed[block, :], wup[...])
 
         def gelu_rows(i, totals):
@@ -449,7 +459,7 @@
                 done.append(totals[q] + sub8(grad))
             return tuple(done)
 
-        bias = lax.fori_loop(0, 4, gelu_rows, tuple(jnp.zeros((8, 256), F32) for _ in range(3)))
+        bias = lax.fori_loop(0, 4, gelu_rows, tuple(jnp.zeros((8, 256), F32) for _ in range(3)), unroll=2)
         dnorm[...] = dot(dpre[block, :], wup[...], (1, 1))
 
         def back_rows(i, totals):
@@ -470,7 +480,7 @@
             return totals[0] + sub8(product), totals[1] + sub8(grad)
 
         zero = jnp.zeros((8, CH), F32)
-        return bias, lax.fori_loop(0, 4, back_rows, (zero, zero))
+        return bias, lax.fori_loop(0, 4, back_rows, (zero, zero), unroll=True)
 
     @pl.when(bottom)
     def _():
@@ -497,6 +507,7 @@
     @pl.when(top)
     def _():
         fold_first(1, dcb[5:8].reshape(96, CH))
+        fold_start(1, 0)
 
     def tap_tile(ct, _):
         lanes = pl.ds(pl.multiple_of(ct * 128, 128), 128)
@@ -560,6 +571,10 @@
         down.start()
         along += [up, down]
 
+    @pl.when(top)
+    def _():
+        fold_next(1, 1)
+
     def put_back(ct, lanes, j, value):
         value = cs[j, :, lanes].astype(F32) + value
         gs_out[j, :, lanes] = value.astype(BF16)
@@ -619,10 +634,6 @@
         up.start()
         down.start()
         along += [up, down]
-
-    @pl.when(top)
-    def _():
-        fold_next(1, 1)
 
     for copy in along:
         copy.wait()
@@ -646,12 +657,6 @@
         copy.start()
         along.append(copy)
 
-    fourth = rows_arrived(dwide, third, dv, ew, ee, es, er)
-
-    @pl.when(top)
-    def _():
-        dwide[:, ROWS + PAD :] = jnp.zeros((3, PAD, WIDE, 128), F32)
-
     @pl.when(top)
     def _():
         fold_next(1, 2)
@@ -667,6 +672,12 @@
         copy = remote(b1.at[:, mine_y], b1.at[:, mine_y], gy_s.at[d - 1], gy_r.at[d - 1], peer_y(d))
         copy.start()
         gather.append(copy)
+
+    fourth = rows_arrived(dwide, third, dv, ew, ee, es, er)
+
+    @pl.when(top)
+    def _():
+        dwide[:, ROWS + PAD :] = jnp.zeros((3, PAD, WIDE, 128), F32)
 
     for copy in gather:
         copy.wait()

time: 93.6 us -> 86.9 us (0.928)
  Pallas kernels: 92.1 us -> 85.4 us
    pallas_call x1, Pallas kernels: 90.4 us -> 83.7 us  [fused(): pl.pallas_call(body, out_shape=[sds((ROWS, COLS, CH), BF16), sds((16, 128...]
where the time goes in v4:
time: 86.9 us; the launch traced here: 86.7 us
  Pallas kernels  85.4 us (98%)
  between operations  1.29 us (1%)
    pallas_call x1, Pallas kernels, fused(): pl.pallas_call(body, out_shape=[sds((ROWS, COLS, CH), BF16), sds((16, 128...  83.7 us

profile of v4, /device:TPU:1, one launch (start us, length us, event | category | flops | bytes accessed | tf_op | source)
XLA Modules:
  0.0 86.7 jit_solution(10906458315361227910)
XLA Ops:
  1.3 83.7 %block.1 = (bf16[8,32,384]{2,1,0:T(8,128)(2,1)}, f32[16,128]{1,0:T(8,128)}, f32[64,512]{1,0:T(8,128)}) custom-call(bf16[8,32,384]{2,1,0:T(8,128)(2,1)} %state.1, bf16[8,32,384]{2,1,0:T(8,128)(2,1)} %cot.1, s32[8,32]{1,0:T(8,128)} %ocean.1, s32[1,1]{1,0:T(1,128)} %bitcast.3.partner, f32[49,384]{1,0:T(8,128)} %taps_in.1, f32[384]{0:T(512)} %gain_in.1, ...), custom_call_target="tpu_custom_call" | custom-call | tf_op jit(solution)/shard_map/block/pallas_call | solution.py:773
  85.0 1.7 %outputs.1 = (bf16[8,32,384]{2,1,0:T(8,128)(2,1)}, f32[12,48]{1,0:T(8,128)}, f32[12,48]{1,0:T(8,128)}, f32[49,384]{1,0:T(8,128)}, f32[4,384]{1,0:T(4,128)}, /*index=5*/f32[768]{0:T(1024)}) custom-call(bf16[8,32,384]{2,1,0:T(8,128)(2,1)} %get-tuple-element.15.gs_in, f32[16,128]{1,0:T(8,128)} %get-tuple-element.16.tile_in, f32[64,512]{1,0:T(8,128)} %get-tuple-element.17.small_in), custom_call_target="tpu_custom_call" | custom-call | tf_op jit(solution)/shard_map/outputs/pallas_call | solution.py:795

commit v5 on v4

--- a/solution.py
+++ b/solution.py
@@ -124,9 +124,9 @@
     wide, dwide, edge, acc, bacc, edge_rows, wup, wdown, bup,
     unit, rstd, normed, masked, dbr, dhid, pre, hidden, dpre, dnorm, dcv, dcb,
     g, gc, h, h1, h2, r2, t, tz, perm,
-    s, sc, s1, sx, s2, sy, s3, sz, b1, b2, b3, fold,
+    s, sc, s1, sx, s3, sz, b2, b3, fold,
     loc, hs, hr, qs, qr, ds, dr, es, er, cs_s, cs_r, f_s, f_r, k_s, k_r, z_s, z_r,
-    sa_s, sa_r, sx_s, sx_r, sy_s, sy_r, sz_s, sz_r, gy_s, gy_r, gx_s, gx_r, gc_s, gc_r, fold_s, fold_r,
+    sa_s, sa_r, sx_s, sx_r, sz_s, sz_r, gx_s, gx_r, gc_s, gc_r, fold_s, fold_r,
 ):
     ia, ja = lax.axis_index("ia"), lax.axis_index("ja")
     x, zl, c = ia // 16, lax.rem(ia // 2, 8), lax.rem(ia, 2)
@@ -153,6 +153,9 @@
 
     def peer_z(d):
         return place(x, y, lax.rem(z + d, 16), c)
+
+    def peer_xy(d):
+        return place(lax.rem(x + d // 4, 4), lax.rem(y + d % 4, 4), z, c)
 
     def peer_u(d):
         to = lax.rem(u + d, 8)
@@ -194,9 +197,8 @@
 
     for d in range(1, 16):
         greet(peer_z(d))
-    for d in range(1, 4):
-        greet(peer_x(d))
-        greet(peer_y(d))
+    for d in range(1, 16):
+        greet(peer_xy(d))
     greet(other)
 
     for load in loads:
@@ -307,7 +309,7 @@
     def _():
         fold_first(0, xs[4:7].reshape(96, CH))
 
-    pl.semaphore_wait(barrier, 26 + jnp.where(top, 14, 0))
+    pl.semaphore_wait(barrier, 35 + jnp.where(top, 14, 0))
 
     def halo(src, w, e, v, send, recv):
         return (
@@ -459,7 +461,7 @@
                 done.append(totals[q] + sub8(grad))
             return tuple(done)
 
-        bias = lax.fori_loop(0, 4, gelu_rows, tuple(jnp.zeros((8, 256), F32) for _ in range(3)), unroll=2)
+        bias = lax.fori_loop(0, 4, gelu_rows, tuple(jnp.zeros((8, 256), F32) for _ in range(3)), unroll=True)
         dnorm[...] = dot(dpre[block, :], wup[...], (1, 1))
 
         def back_rows(i, totals):
@@ -553,8 +555,10 @@
     mine_s = pl.multiple_of(c * 32, 32)
     s1[...] = (s[pl.ds(mine_s, 32), :] + sc[...]).reshape(4, 8, 512)
     small = []
-    for d in range(1, 4):
-        copy = remote(s1.at[lax.rem(x + d, 4)], sx.at[d - 1], sx_s.at[d - 1], sx_r.at[d - 1], peer_x(d))
+    for d in range(1, 16):
+        chunk = pl.ds(pl.multiple_of(lax.rem(y + d % 4, 4) * 128, 128), 128)
+        piece = s1.at[lax.rem(x + d // 4, 4), :, chunk]
+        copy = remote(piece, sx.at[d - 1], sx_s.at[d - 1], sx_r.at[d - 1], peer_xy(d))
         copy.start()
         small.append(copy)
 
@@ -594,23 +598,11 @@
 
     for copy in small:
         copy.wait()
-    s2[...] = s1[x] + sx[0] + sx[1] + sx[2]
-    small = []
-    for d in range(1, 4):
-        chunk = pl.ds(pl.multiple_of(lax.rem(y + d, 4) * 128, 128), 128)
-        copy = remote(s2.at[:, chunk], sy.at[d - 1], sy_s.at[d - 1], sy_r.at[d - 1], peer_y(d))
-        copy.start()
-        small.append(copy)
-
-    for copy in third[2:]:
-        copy.wait()
-    widen_sides(dwide, dw, de)
-    conv_part(dwide, taps, True, own, every, nothing, write_bacc)
-
-    for copy in small:
-        copy.wait()
     mine_y = pl.ds(pl.multiple_of(y * 128, 128), 128)
-    s3[...] = s2[:, mine_y] + sy[0] + sy[1] + sy[2]
+    total = s1[x, :, mine_y]
+    for q in range(15):
+        total = total + sx[q]
+    s3[...] = total
     small = []
     for d in range(1, 16):
         copy = remote(s3, sz.at[z], sz_s.at[d - 1], sz_r.at[d - 1], peer_z(d))
@@ -634,6 +626,11 @@
         up.start()
         down.start()
         along += [up, down]
+
+    for copy in third[2:]:
+        copy.wait()
+    widen_sides(dwide, dw, de)
+    conv_part(dwide, taps, True, own, every, nothing, write_bacc)
 
     for copy in along:
         copy.wait()
@@ -666,10 +663,11 @@
     total = sz[0]
     for q in range(1, 16):
         total = total + sz[q]
-    b1[:, mine_y] = total * FACTOR
+    b2[x, :, mine_y] = total * FACTOR
     gather = []
-    for d in range(1, 4):
-        copy = remote(b1.at[:, mine_y], b1.at[:, mine_y], gy_s.at[d - 1], gy_r.at[d - 1], peer_y(d))
+    for d in range(1, 16):
+        piece = b2.at[x, :, mine_y]
+        copy = remote(piece, piece, gx_s.at[d - 1], gx_r.at[d - 1], peer_xy(d))
         copy.start()
         gather.append(copy)
 
@@ -678,15 +676,6 @@
     @pl.when(top)
     def _():
         dwide[:, ROWS + PAD :] = jnp.zeros((3, PAD, WIDE, 128), F32)
-
-    for copy in gather:
-        copy.wait()
-    b2[x] = b1[...]
-    gather = []
-    for d in range(1, 4):
-        copy = remote(b1, b2.at[x], gx_s.at[d - 1], gx_r.at[d - 1], peer_x(d))
-        copy.start()
-        gather.append(copy)
 
     @pl.when(top)
     def _():
@@ -762,13 +751,13 @@
         vm((2, 2, 384, 384), BF16), vm((2, 384, 384), BF16), vm((2, 4, 96, 384), BF16),
         vm((2, 3, 96, 384), BF16), vm((2, 4, 96, 128), BF16), vm((2, 3, 96, 128), BF16),
         vm((16, 16, 128), BF16), vm((15, 16, 128), BF16), vm((HID, HID), BF16),
-        vm((64, 512), F32), vm((32, 512), F32), vm((4, 8, 512), F32), vm((3, 8, 512), F32), vm((8, 512), F32),
-        vm((3, 8, 128), F32), vm((8, 128), F32), vm((16, 8, 128), F32), vm((8, 512), F32), vm((4, 8, 512), F32),
+        vm((64, 512), F32), vm((32, 512), F32), vm((4, 8, 512), F32), vm((15, 8, 128), F32),
+        vm((8, 128), F32), vm((16, 8, 128), F32), vm((4, 8, 512), F32),
         vm((2, 4, 8, 512), F32), vm((2, 4, 2, 8, 16, CH), BF16),
         dma((12,)), dma((4,)), dma((4,)), dma((4,)), dma((4,)), dma((4,)), dma((4,)), dma((4,)), dma((4,)),
         dma((1,)), dma((1,)), dma((2, 3)), dma((2, 3)), dma((2, 3)), dma((2, 3)), dma((15,)), dma((15,)),
-        dma((1,)), dma((1,)), dma((3,)), dma((3,)), dma((3,)), dma((3,)), dma((15,)), dma((15,)),
-        dma((3,)), dma((3,)), dma((3,)), dma((3,)), dma((1,)), dma((1,)), dma((2, 4, 7)), dma((2, 4, 7)),
+        dma((1,)), dma((1,)), dma((15,)), dma((15,)), dma((15,)), dma((15,)),
+        dma((15,)), dma((15,)), dma((1,)), dma((1,)), dma((2, 4, 7)), dma((2, 4, 7)),
     ]
     return pl.pallas_call(
         body,

time: 86.9 us -> 84.5 us (0.972)
  Pallas kernels: 85.4 us -> 83.1 us
    pallas_call x1, Pallas kernels: 83.7 us -> 81.3 us  [fused(): pl.pallas_call(body, out_shape=[sds((ROWS, COLS, CH), BF16), sds((16, 128...]
where the time goes in v5:
time: 84.5 us; the launch traced here: 84.4 us
  Pallas kernels  83.1 us (98%)
  between operations  1.29 us (2%)
    pallas_call x1, Pallas kernels, fused(): pl.pallas_call(body, out_shape=[sds((ROWS, COLS, CH), BF16), sds((16, 128...  81.3 us
    pallas_call x1, Pallas kernels, local(): pl.pallas_call(finish, out_shape=[sds((ROWS, COLS, CH), BF16), sds((12, 4...  1.74 us

profile of v5, /device:TPU:1, one launch (start us, length us, event | category | flops | bytes accessed | tf_op | source)
XLA Modules:
  0.0 84.4 jit_solution(16839204661814895397)
XLA Ops:
  1.3 81.3 %block.1 = (bf16[8,32,384]{2,1,0:T(8,128)(2,1)}, f32[16,128]{1,0:T(8,128)}, f32[64,512]{1,0:T(8,128)}) custom-call(bf16[8,32,384]{2,1,0:T(8,128)(2,1)} %state.1, bf16[8,32,384]{2,1,0:T(8,128)(2,1)} %cot.1, s32[8,32]{1,0:T(8,128)} %ocean.1, s32[1,1]{1,0:T(1,128)} %bitcast.3.partner, f32[49,384]{1,0:T(8,128)} %taps_in.1, f32[384]{0:T(512)} %gain_in.1, ...), custom_call_target="tpu_custom_call" | custom-call | tf_op jit(solution)/shard_map/block/pallas_call | solution.py:762
  82.6 1.7 %outputs.1 = (bf16[8,32,384]{2,1,0:T(8,128)(2,1)}, f32[12,48]{1,0:T(8,128)}, f32[12,48]{1,0:T(8,128)}, f32[49,384]{1,0:T(8,128)}, f32[4,384]{1,0:T(4,128)}, /*index=5*/f32[768]{0:T(1024)}) custom-call(bf16[8,32,384]{2,1,0:T(8,128)(2,1)} %get-tuple-element.15.gs_in, f32[16,128]{1,0:T(8,128)} %get-tuple-element.16.tile_in, f32[64,512]{1,0:T(8,128)} %get-tuple-element.17.small_in), custom_call_target="tpu_custom_call" | custom-call | tf_op jit(solution)/shard_map/outputs/pallas_call | solution.py:784
